TPU v7x, 128 devices: a whole 4x4x4 slice. The times are simulated.
128 devices in a mesh: ctx: 32 (over z, x, y_lo), kvh: 4 (over y_hi, core).
Axes of the slice: x: 4, y: 4 (y_hi: 2, y_lo: 2; y = y_hi * 2 + y_lo), z: 4, core: 2. Of those that a mesh axis runs over, the one named last changes fastest.
Arguments:
- span_queries: bfloat16 [4096, 12288], P('ctx', 'kvh'), may hold values from -8 to 8, as said below
- span_keyvals: bfloat16 [2, 4096, 1024], P(None, 'ctx', 'kvh'), may hold values from -6 to 6
- prefix_keyvals: bfloat16 [2, 2048, 1024], P(None, ('ctx', 'kvh')), may hold values from -6 to 6
- offset: int32 [1], replicated, may hold values from 1024 to 2048
- decode_queries: bfloat16 [32, 12288], replicated, may hold values from -8 to 8
- private_keyvals: bfloat16 [2, 32, 1024, 1024], P(None, None, ('ctx', 'kvh')), may hold values from -6 to 6
- suffix_lengths: int32 [32], replicated, may hold values from 1 to 1024
- out_weight: bfloat16 [12288, 12288], P('kvh', 'ctx'), may hold values from -0.0546875 to 0.0546875
Outputs:
- span_attention: float32 [4096, 12288], P('ctx', 'kvh')
- relaid_span: bfloat16 [2, 4096, 1024], P(None, ('ctx', 'kvh'))
- decode_output: float32 [32, 12288], P(None, 'ctx')
Inputs may be any that keep to these rules, and one draw needn't show every extreme that they name: `span_queries`: query entries.
All inputs are finite; a program needn't handle non-finite values.
Results may differ from a plain program's by a relative error of at most 0.007.
Values may be sent and summed in bfloat16 or wider, within the bound.
A program may use at most 768 MiB of HBM per device.

v0:
```python
import math

import jax
import jax.numpy as jnp
from jax import lax
from jax.sharding import PartitionSpec as P

H = 96
KVH = 8
HD = 128


masked_score = -1e30


def fold_block(carry, queries, keys, values, allowed):
    maxima, totals, weighted = carry
    scores = jnp.einsum(
        "qhgd,khd->hgqk", queries, keys, preferred_element_type=jnp.float32
    ) * HD ** (-0.5)
    scores = jnp.where(allowed[None, None], scores, masked_score)
    larger = jnp.maximum(maxima, jnp.max(scores, axis=-1))
    rescale = jnp.exp(maxima - larger)
    weights = jnp.where(allowed[None, None], jnp.exp(scores - larger[..., None]), 0.0).astype(
        jnp.bfloat16
    )
    totals = totals * rescale + jnp.sum(weights.astype(jnp.float32), axis=-1)
    update = jnp.einsum("hgqk,khd->qhgd", weights, values, preferred_element_type=jnp.float32)
    weighted = weighted * jnp.transpose(rescale, (2, 0, 1))[..., None] + update
    return (larger, totals, weighted)


def sweep_piece(carry, queries, piece, start, allowed_for):
    piece_rows = piece.shape[1]
    block_rows = math.gcd(piece_rows, 512)
    heads_here = queries.shape[1]

    def advance(block_index, state):
        part = lax.dynamic_slice_in_dim(piece, block_index * block_rows, block_rows, 1)
        keys = part[0].reshape(block_rows, heads_here, HD)
        values = part[1].reshape(block_rows, heads_here, HD)
        positions = start + block_index * block_rows + jnp.arange(block_rows, dtype=jnp.int32)
        return fold_block(state, queries, keys, values, allowed_for(positions))

    return lax.fori_loop(0, piece_rows // block_rows, advance, carry)


def shards(
    span_queries,
    span_keyvals,
    prefix_keyvals,
    offset,
    decode_queries,
    private_keyvals,
    suffix_lengths,
    out_weight,
):
    limit = offset[0]
    query_rows = span_queries.shape[0]
    head_width = span_keyvals.shape[2]
    heads_here = head_width // HD
    per_group = H // KVH
    queries = span_queries.reshape(query_rows, heads_here, per_group, HD)
    query_pos = lax.axis_index("ctx") * query_rows + jnp.arange(query_rows, dtype=jnp.int32)

    def prefix_allowed(positions):
        return jnp.broadcast_to((positions < limit)[None, :], (query_rows, positions.shape[0]))

    def span_allowed(positions):
        return positions[None, :] <= query_pos[:, None]

    start_state = (
        jnp.full((heads_here, per_group, query_rows), masked_score, jnp.float32),
        jnp.zeros((heads_here, per_group, query_rows), jnp.float32),
        jnp.zeros((query_rows, heads_here, per_group, HD), jnp.float32),
    )
    relaid = lax.all_to_all(prefix_keyvals, "kvh", split_axis=2, concat_axis=1, tiled=True)
    group_prefix = lax.all_gather(relaid, "ctx", axis=1, tiled=True)
    state = sweep_piece(start_state, queries, group_prefix, 0, prefix_allowed)
    maxima, totals, weighted = sweep_piece(
        state,
        queries,
        lax.all_gather(span_keyvals, "ctx", axis=1, tiled=True),
        jnp.int32(0),
        span_allowed,
    )
    span_attention = (weighted / jnp.transpose(totals, (2, 0, 1))[..., None]).reshape(
        query_rows, -1
    )
    relaid_span = lax.all_to_all(span_keyvals, "kvh", split_axis=1, concat_axis=2, tiled=True)
    samples = decode_queries.shape[0]
    flat_index = lax.axis_index(("ctx", "kvh"))
    prefix_rows = prefix_keyvals.shape[1]
    shared = jnp.concatenate([prefix_keyvals, relaid_span], axis=1)
    shared_rows = shared.shape[1]
    shared_keys = shared[0].reshape(shared_rows, KVH, HD)
    shared_values = shared[1].reshape(shared_rows, KVH, HD)
    private_rows = private_keyvals.shape[2]
    private_keys = private_keyvals[0].reshape(samples, private_rows, KVH, HD)
    private_values = private_keyvals[1].reshape(samples, private_rows, KVH, HD)
    sample_queries = decode_queries.reshape(samples, KVH, per_group, HD)
    shared_scores = jnp.einsum(
        "bhgd,khd->bhgk", sample_queries, shared_keys, preferred_element_type=jnp.float32
    )
    private_scores = jnp.einsum(
        "bhgd,brhd->bhgr", sample_queries, private_keys, preferred_element_type=jnp.float32
    )
    scores = jnp.concatenate([shared_scores, private_scores], axis=-1) * HD ** (-0.5)
    shared_pos = flat_index * prefix_rows + jnp.arange(shared_rows, dtype=jnp.int32)
    shared_ok = jnp.logical_or(
        shared_pos < limit, jnp.arange(shared_rows, dtype=jnp.int32) >= prefix_rows
    )
    private_pos = flat_index * private_rows + jnp.arange(private_rows, dtype=jnp.int32)
    private_ok = private_pos[None, :] < suffix_lengths[:, None]
    allowed = jnp.concatenate(
        [jnp.broadcast_to(shared_ok[None, :], (samples, shared_rows)), private_ok], axis=1
    )[:, None, None, :]
    scores = jnp.where(allowed, scores, masked_score)
    sample_max = jnp.max(scores, axis=-1)
    weights = jnp.where(allowed, jnp.exp(scores - sample_max[..., None]), 0.0).astype(jnp.bfloat16)
    sample_total = jnp.sum(weights.astype(jnp.float32), axis=-1)
    sample_sum = jnp.einsum(
        "bhgk,khd->bhgd",
        weights[..., :shared_rows],
        shared_values,
        preferred_element_type=jnp.float32,
    )
    sample_sum = sample_sum + jnp.einsum(
        "bhgr,brhd->bhgd",
        weights[..., shared_rows:],
        private_values,
        preferred_element_type=jnp.float32,
    )
    sample_max = sample_max.reshape(samples, H)
    sample_total = sample_total.reshape(samples, H)
    sample_sum = sample_sum.reshape(samples, H * HD)
    slice_width = out_weight.shape[0]
    slice_heads = slice_width // HD
    highest = lax.pmax(sample_max, ("ctx", "kvh"))
    factor = jnp.exp(sample_max - highest)
    scaled = (sample_sum.reshape(samples, H, HD) * factor[..., None]).reshape(samples, H * HD)
    share_sum, share_total = (
        lax.psum_scatter(scaled, "kvh", scatter_dimension=1, tiled=True),
        lax.psum_scatter(sample_total * factor, "kvh", scatter_dimension=1, tiled=True),
    )
    own_sum, own_total = lax.psum((share_sum, share_total), "ctx")
    mixed = (
        (own_sum.reshape(samples, slice_heads, HD) / own_total[..., None])
        .reshape(samples, slice_width)
        .astype(jnp.bfloat16)
    )
    partial_out = jnp.dot(mixed, out_weight, preferred_element_type=jnp.float32)
    decode_output = lax.psum(partial_out, "kvh")
    return (span_attention, relaid_span, decode_output)


def solution(mesh):
    return jax.shard_map(
        shards,
        mesh=mesh,
        in_specs=(
            P("ctx", "kvh"),
            P(None, "ctx", "kvh"),
            P(None, ("ctx", "kvh"), None),
            P(),
            P(),
            P(None, None, ("ctx", "kvh"), None),
            P(),
            P("kvh", "ctx"),
        ),
        out_specs=(P("ctx", "kvh"), P(None, ("ctx", "kvh"), None), P(None, "ctx")),
        check_vma=False,
    )
```

profile of v0, /device:TPU:0, one launch (start us, length us, event | category | flops | bytes accessed | tf_op | source)
XLA Modules:
  0.0 846.6 jit_solution(4904664648153168351)
XLA Ops:
  9.0 4.5 all-to-all-start.1
  17.9 4.3 copy.80
  37.2 2.8 reshape_reshape.3
  40.0 69.1 %pmax.7 = f32[32,96]{0,1:T(8,128)S(1)} all-reduce(f32[32,96]{0,1:T(8,128)S(1)} %reshape.86), channel_id=1, replica_groups=mesh['ctx'=32,'kvh'=4] {'ctx','kvh'}, use_global_device_ids=true, to_apply=%region_9.10 | all-reduce | flops 3072 | bytes 24576 | tf_op jit(solution)/shard_map/pmax | solution.py:139
  114.1 30.7 %reduce-scatter.5.cloned.1.call-done = f32[32,3072]{1,0:T(8,128)} async-done(((f32[32,12288]{1,0:T(8,128)}), f32[32,3072]{1,0:T(8,128)}) %reduce-scatter.5.cloned.1.call-update) | async-done | bytes 393232 | tf_op jit(solution)/shard_map/reduce_scatter | solution.py:143
  145.8 8.0 all_to_all.36
  159.9 13.9 %reduce-scatter.7.cloned.1.call-done = f32[32,24]{0,1:T(8,128)} async-done(((f32[32,96]{0,1:T(8,128)}), f32[32,24]{0,1:T(8,128)}) %reduce-scatter.7.cloned.1.call-update) | async-done | bytes 3088
  173.8 157.2 %psum.22 = f32[32,24]{0,1:T(8,128)S(1)} all-reduce(f32[32,24]{0,1:T(8,128)} %reduce-scatter.7.cloned.1.call-done), channel_id=1, replica_groups=mesh['ctx'=32,'kvh'=4] {'ctx'}, use_global_device_ids=true, to_apply=%region_14.15 | all-reduce | flops 768 | bytes 6144 | tf_op jit(solution)/shard_map/psum | solution.py:146
  331.1 137.8 %all-reduce.3.cloned.1.call-done = f32[32,3072]{1,0:T(8,128)} async-done(((f32[32,3072]{1,0:T(8,128)}), f32[32,3072]{1,0:T(8,128)}) %all-reduce.3.cloned.1.call-update) | async-done | bytes 393232 | tf_op jit(solution)/shard_map/psum | solution.py:146
  470.5 14.2 %psum.23 = f32[32,384]{1,0:T(8,128)} all-reduce(f32[32,384]{1,0:T(8,128)S(1)} %fusion.21), channel_id=1, replica_groups=mesh['ctx'=32,'kvh'=4] {'kvh'}, use_global_device_ids=true, to_apply=%region_15.16 | all-reduce | flops 12288 | bytes 98304 | tf_op jit(solution)/shard_map/psum | solution.py:153
  484.7 136.0 %all-gather.3.cloned.1.call-done = bf16[2,2048,256]{2,1,0:T(8,128)(2,1)} async-done(((bf16[2,64,256]{2,1,0:T(8,128)(2,1)}), bf16[2,2048,256]{2,1,0:T(8,128)(2,1)}) %all-gather.3.cloned.1.call-update) | async-done | bytes 2097168 | tf_op jit(solution)/shard_map/all_gather | solution.py:78
  620.7 60.5 %while.37 = (s32[]{:T(128)}, f32[2,12,128]{2,1,0:T(8,128)S(1)}, f32[2,12,128]{2,1,0:T(8,128)S(1)}, f32[128,2,12,128]{0,3,2,1:T(8,128)}, s32[]{:T(128)}, /*index=...) while((s32[]{:T(128)}, f32[2,12,128]{2,1,0:T(8,128)S(1)}, ...), condition=%wide.region_3.4_spmd.clone, body=%wide.region_0.3_spmd.clone.sunk | while | flops 822234112 | bytes 25614032 | solution.py:45
  627.5 3.3 convert_reduce_fusion.6
  631.7 3.8 bitcast_add_fusion.6
  642.3 3.3 convert_reduce_fusion.6
  646.5 4.3 bitcast_add_fusion.6
  657.6 3.3 convert_reduce_fusion.6
  661.7 4.2 bitcast_add_fusion.6
  672.8 3.3 convert_reduce_fusion.6
  677.0 4.3 bitcast_add_fusion.6
  681.2 95.9 %all-gather.5.cloned.1.call-done = bf16[2,4096,256]{1,2,0:T(8,128)(2,1)} async-done(((bf16[2,128,256]{1,2,0:T(8,128)(2,1)}), bf16[2,4096,256]{1,2,0:T(8,128)(2,1)}) %all-gather.5.cloned.1.call-update) | async-done | bytes 4194320 | tf_op jit(solution)/shard_map/all_gather | solution.py:83
  777.2 57.1 %while.36 = (s32[]{:T(128)}, f32[2,12,128]{2,1,0:T(8,128)S(1)}, f32[2,12,128]{2,1,0:T(8,128)S(1)}, f32[128,2,12,128]{0,3,2,1:T(8,128)}, bf16[2,4096,256]{1,2,0:T...) while((s32[]{:T(128)}, f32[2,12,128]{2,1,0:T(8,128)S(1)}, ...), condition=%wide.region_7.8_spmd.clone, body=%wide.region_4.7_spmd.clone.sunk | while | flops 829761152 | bytes 37426432 | solution.py:45
  834.2 2.8 broadcast_divide_fusion
  837.0 3.0 copy.87
  (215 shorter events, 121.1 us)
Async XLA Ops:
  7.2 461.9 %copy-start = (bf16[3072,384]{1,0:T(8,128)(2,1)S(1)}, bf16[3072,384]{1,0:T(8,128)(2,1)}, u32[]{:S(2)}) copy-start(bf16[3072,384]{1,0:T(8,128)(2,1)} %param.19) | copy-start | bytes 7077892
  9.0 15.5 %all-to-all-start.1 = ((bf16[2,128,256]{2,0,1:T(2,128)(2,1)}), bf16[2,128,256]{2,0,1:T(2,128)(2,1)S(1)}, u32[]{:S(2)}, u32[]{:S(2)}) async-start(bf16[2,128,256]{2,0,1:T(2,128)(2,1)} %copy.76), calls=%async_computation.1 | async-start | bytes 262144 | tf_op jit(solution)/shard_map/all_to_all | solution.py:90
  13.6 131.2 %reduce-scatter.5.cloned.1.call-start = ((), (), s32[]{:S(2)}) async-start(), calls=%async_computation.6 | async-start | bytes 1966080 | tf_op jit(solution)/shard_map/reduce_scatter | solution.py:143
  17.9 4.9 copy-start.10
  26.3 3.0 copy-start.7
  27.0 2.3 copy-start.3
  31.7 1.2 copy-start.5
  109.8 1.4 copy-start.4
  113.3 31.6 %copy-start.9 = (bf16[2,16,1024]{2,1,0:T(8,128)(2,1)S(1)}, bf16[2,16,1024]{2,1,0:T(8,128)(2,1)}, u32[]{:S(2)}) copy-start(bf16[2,16,1024]{2,1,0:T(8,128)(2,1)} %param.14) | copy-start | bytes 196612
  113.3 60.5 %reduce-scatter.7.cloned.1.call-start = ((), (), s32[]{:S(2)}) async-start(), calls=%async_computation.8 | async-start | bytes 61440
  113.4 41.9 %copy-start.6 = (bf16[2,128,256]{2,1,0:T(8,128)(2,1)S(1)}, bf16[2,128,256]{2,1,0:T(8,128)(2,1)}, u32[]{:S(2)}) copy-start(bf16[2,128,256]{2,1,0:T(8,128)(2,1)} %param.13) | copy-start | bytes 393220
  114.1 354.8 %all-reduce.3.cloned.1.call-start = ((), (), s32[]{:S(2)}) async-start(), calls=%async_computation.7 | async-start | bytes 786432 | tf_op jit(solution)/shard_map/psum | solution.py:146
  144.8 475.9 %all-gather.3.cloned.1.call-start = ((), (), s32[]{:S(2)}) async-start(), calls=%async_computation.4 | async-start | bytes 2162688 | tf_op jit(solution)/shard_map/all_gather | solution.py:78
  155.3 621.9 %all-gather.5.cloned.1.call-start = ((), (), s32[]{:S(2)}) async-start(), calls=%async_computation.5 | async-start | bytes 4325376 | tf_op jit(solution)/shard_map/all_gather | solution.py:83
  779.6 1.6 copy-start.1
  783.2 1.1 copy-start.2
  786.7 1.6 copy-start.1
  793.8 1.6 copy-start.1
  801.0 1.6 copy-start.1
  808.1 1.6 copy-start.1
  815.2 1.6 copy-start.1
  818.8 1.1 copy-start.2
  822.4 1.6 copy-start.1
  829.5 1.6 copy-start.1
  (7 other events, 7.8 us)
Sparse Core Ops, SparseCore 0:
  113.4 31.3 reduce-scatter.4
  148.1 25.6 reduce-scatter.6
  176.3 292.5 all-reduce.2
  470.5 150.1 all-gather.2
  622.2 154.8 all-gather.4
where the time goes:
time: 850 us; the launch traced here: 847 us
  waiting for transfers between devices  415 us (49%)
  blocking collectives  249 us (29%)
  local copies, waits for them, and re-layouts  67.3 us (8%)
  matrix products  58.1 us (7%)
  other arithmetic  37.4 us (4%)
  between operations  14.7 us (2%)
    psum x1, blocking collectives, shards(): own_sum, own_total = lax.psum((share_sum, share_total), 'ctx')  157 us
    psum x1, waiting for transfers between devices, shards(): own_sum, own_total = lax.psum((share_sum, share_total), 'ctx')  138 us
    all_gather x1, waiting for transfers between devices, shards(): group_prefix = lax.all_gather(relaid, 'ctx', axis=1, tiled=True)  136 us
    all_gather x1, waiting for transfers between devices, shards(): lax.all_gather(span_keyvals, 'ctx', axis=1, tiled=True)  95.9 us
    pmax x1, blocking collectives, shards(): highest = lax.pmax(sample_max, ('ctx', 'kvh'))  69.1 us
    dot_general x12, matrix products, fold_block(): jnp.einsum('hgqk,khd->qhgd', weights, values, preferred_element_type=jnp....  32.7 us
    reduce_scatter x1, waiting for transfers between devices, shards(): lax.psum_scatter(scaled, 'kvh', scatter_dimension=1, tiled=True)  30.7 us
    reduce_sum x12, other arithmetic, fold_block(): totals = totals * rescale + jnp.sum(weights.astype(jnp.float32), axis=-1)  25.3 us
  transfers between devices with their start and end apart: 6, of which 5 were waited for; matrix products, arithmetic and copies ran while one was open for 9% of the time, Pallas kernels for 0%

commit v1 on v0

v1 whole, which is shorter than its diff:
```python
import jax
import jax.numpy as jnp
from jax import lax
from jax.experimental import pallas as pl
from jax.experimental.pallas import tpu as pltpu
from jax.sharding import PartitionSpec as P

H = 96
KVH = 8
HD = 128
CTX = 32
GROUPS = 4
SAMPLES = 32
PER = H // KVH
PAD = 16
SPAN_ROWS = 128
PRE_ROWS = 64
ROWS = SPAN_ROWS + PRE_ROWS
PREFIX = 2048
LOG2E = 1.4426950408889634
SCALE = HD ** (-0.5) * LOG2E
MASKED = -1e30

MESH = pl.DeviceIdType.MESH
F32 = jnp.float32
BF16 = jnp.bfloat16


def rem(a, n):
    return lax.rem(a, jnp.int32(n))


def dot_t(a, b):
    return lax.dot_general(a, b, (((1,), (1,)), ((), ())), preferred_element_type=F32)


def dot(a, b):
    return jnp.dot(a, b, preferred_element_type=F32)


def remote(src, dst, send, recv, device):
    return pltpu.make_async_remote_copy(
        src_ref=src, dst_ref=dst, send_sem=send, recv_sem=recv, device_id=device, device_id_type=MESH
    )


def greet(devices):
    barrier = pltpu.get_barrier_semaphore()
    for device in devices:
        pl.semaphore_signal(barrier, inc=1, device_id=device, device_id_type=MESH)
    pl.semaphore_wait(barrier, len(devices))


def decode_kernel(
    limit_ref, suffix_ref, span_ref, prefix_ref, private_ref, dq_ref, w_ref,
    prefix_out, relaid_out, decode_out,
    w_buf, q_buf, qf, priv, suf, msg, inbox, mix_own, mix_all, mix_f, part, parts,
    w_sem, dq_sem, kv_send, kv_recv, own_sem, in_send, in_recv, mix_send, mix_recv, part_send, part_recv,
):
    c = lax.axis_index("ctx")
    g = lax.axis_index("kvh")
    limit = limit_ref[0]
    width = 2 * HD

    w_copy = pltpu.make_async_copy(w_ref, w_buf, w_sem)
    w_copy.start()
    dq_copy = pltpu.make_async_copy(
        dq_ref.at[:, pl.ds(pl.multiple_of(g * 2 * PER * HD, HD), 2 * PER * HD)], q_buf, dq_sem
    )
    dq_copy.start()

    barrier = pltpu.get_barrier_semaphore()
    for k in range(1, GROUPS):
        pl.semaphore_signal(barrier, inc=1, device_id=(c, rem(g + k, GROUPS)), device_id_type=MESH)

    def greet_ctx(k, carry):
        pl.semaphore_signal(barrier, inc=1, device_id=(rem(c + k, CTX), g), device_id_type=MESH)
        return carry

    lax.fori_loop(1, CTX, greet_ctx, 0)
    pl.semaphore_wait(barrier, CTX - 1 + GROUPS - 1)

    def columns(which):
        return pl.ds(pl.multiple_of(which * width, width), width)

    def rows_of(which, count):
        return pl.ds(pl.multiple_of(which * count, count), count)

    kv_copies = []
    for k in range(1, GROUPS):
        to = rem(g + k, GROUPS)
        pairs = (
            (prefix_ref.at[:, :, columns(to)], prefix_out.at[:, rows_of(g, 16), :]),
            (private_ref.at[:, :, columns(to)], priv.at[g]),
            (span_ref.at[:, rows_of(to, 32), :], relaid_out.at[:, :, columns(g)]),
        )
        for n, (src, dst) in enumerate(pairs):
            copy = remote(src, dst, kv_send.at[n, k - 1], kv_recv.at[n, k - 1], (c, to))
            copy.start()
            kv_copies.append(copy)
    own_pairs = (
        (prefix_ref.at[:, :, columns(g)], prefix_out.at[:, rows_of(g, 16), :]),
        (private_ref.at[:, :, columns(g)], priv.at[g]),
        (span_ref.at[:, rows_of(g, 32), :], relaid_out.at[:, :, columns(g)]),
    )
    own_copies = []
    for n, (src, dst) in enumerate(own_pairs):
        copy = pltpu.make_async_copy(src, dst, own_sem.at[n])
        copy.start()
        own_copies.append(copy)

    qf[...] = jnp.zeros_like(qf)
    dq_copy.wait()
    for j in range(2 * PER):
        start = (j // PER) * SAMPLES * PAD + j % PER
        qf[pl.ds(start, SAMPLES, stride=PAD), :] = q_buf[:, j * HD : (j + 1) * HD].astype(F32)

    def set_suffix(b, carry):
        suf[pl.ds(pl.multiple_of(b * 8, 8), 8), :] = jnp.full((8, HD), suffix_ref[b], jnp.int32)
        return carry

    lax.fori_loop(0, SAMPLES, set_suffix, 0)

    for copy in own_copies:
        copy.wait()
    for copy in kv_copies:
        copy.wait_recv()

    pre_pos = c * PRE_ROWS + lax.broadcasted_iota(jnp.int32, (PRE_ROWS, HD), 0)
    pre_ok = pre_pos < limit
    row_in = lax.broadcasted_iota(jnp.int32, (8 * SAMPLES, HD), 0)
    one_pre = jnp.where(pre_ok, 1.0, 0.0).astype(BF16)
    ok_priv = [(c * GROUPS + s) * 8 + (row_in & 7) < suf[...] for s in range(GROUPS)]
    keys, values = [], []
    for h in range(2):
        cols = slice(h * HD, (h + 1) * HD)
        sub = span_ref[0, 0:1, cols].astype(F32)
        key_list = [
            span_ref[0, :, cols],
            jnp.where(pre_ok, prefix_out[0, :, cols].astype(F32), sub).astype(BF16),
        ]
        value_list = [
            jnp.concatenate([span_ref[1, :, cols], jnp.ones((SPAN_ROWS, HD), BF16)], axis=1),
            jnp.concatenate(
                [jnp.where(pre_ok, prefix_out[1, :, cols].astype(F32), 0.0).astype(BF16), one_pre], axis=1
            ),
        ]
        for s in range(GROUPS):
            key_list.append(jnp.where(ok_priv[s], priv[s, 0, :, cols].astype(F32), sub).astype(BF16))
            value_list.append(
                jnp.concatenate(
                    [
                        jnp.where(ok_priv[s], priv[s, 1, :, cols].astype(F32), 0.0).astype(BF16),
                        jnp.where(ok_priv[s], 1.0, 0.0).astype(BF16),
                    ],
                    axis=1,
                )
            )
        keys.append(jnp.concatenate(key_list, axis=0))
        values.append(jnp.concatenate(value_list, axis=0))

    tile = 128
    total = ROWS + GROUPS * 8 * SAMPLES

    def partial_tile(t, carry):
        row = t * tile + lax.broadcasted_iota(jnp.int32, (tile, total), 0)
        col = lax.broadcasted_iota(jnp.int32, (tile, total), 1) - ROWS
        match = jnp.logical_or(col < 0, (row >> 4) == ((col >> 3) & (SAMPLES - 1)))
        lane = lax.broadcasted_iota(jnp.int32, (tile, HD), 1)
        stats = jnp.zeros((tile, HD), F32)
        outs = []
        for h in range(2):
            q = qf[pl.ds(pl.multiple_of(h * SAMPLES * PAD + t * tile, tile), tile), :].astype(BF16)
            s = jnp.where(match, dot_t(q, keys[h]) * SCALE, MASKED)
            top = jnp.max(s, axis=1, keepdims=True)
            weights = jnp.exp2(s - top).astype(BF16)
            acc = dot(weights, values[h])
            total_here = acc[:, HD:]
            outs.append((acc[:, :HD] / total_here).astype(BF16))
            lse = top + jnp.log2(total_here)
            high = lse.astype(BF16).astype(F32)
            middle = (lse - high).astype(BF16).astype(F32)
            low = lse - high - middle
            stats = jnp.where(lane == 3 * h, high, stats)
            stats = jnp.where(lane == 3 * h + 1, middle, stats)
            stats = jnp.where(lane == 3 * h + 2, low, stats)
        here = pl.ds(t * (tile // PAD), tile // PAD)
        msg[here, 0, :, :] = outs[0].reshape(tile // PAD, PAD, HD)
        msg[here, 1, :, :] = outs[1].reshape(tile // PAD, PAD, HD)
        msg[here, 2, :, :] = stats.astype(BF16).reshape(tile // PAD, PAD, HD)
        return carry

    lax.fori_loop(0, SAMPLES * PAD // tile, partial_tile, 0)

    def in_copy(k):
        to = rem(c + k, CTX)
        return remote(msg.at[to], inbox.at[k], in_send.at[k], in_recv.at[k], (to, g))

    def start_in(k, carry):
        in_copy(k).start()
        return carry

    def wait_in(k, carry):
        in_copy(k).wait()
        return carry

    lax.fori_loop(1, CTX, start_in, 0)
    inbox[0] = msg[c]
    lax.fori_loop(1, CTX, wait_in, 0)

    stat = inbox[:, 2, :, :].astype(F32)
    for h in range(2):
        lse = stat[:, :, 3 * h : 3 * h + 1] + stat[:, :, 3 * h + 1 : 3 * h + 2] + stat[:, :, 3 * h + 2 : 3 * h + 3]
        weight = jnp.exp2(lse - jnp.max(lse, axis=0, keepdims=True))
        mixed = jnp.sum(weight * inbox[:, h, :, :].astype(F32), axis=0) / jnp.sum(weight, axis=0)
        mix_own[h] = mixed.astype(BF16)

    def mix_copy(k):
        to = rem(c + k, CTX)
        return remote(mix_own, mix_all.at[c], mix_send.at[k], mix_recv.at[k], (to, g))

    def start_mix(k, carry):
        mix_copy(k).start()
        return carry

    def wait_mix(k, carry):
        mix_copy(k).wait()
        return carry

    lax.fori_loop(1, CTX, start_mix, 0)
    mix_all[c] = mix_own[...]
    lax.fori_loop(1, CTX, wait_mix, 0)

    mix_f[...] = mix_all[...].astype(F32).reshape(SAMPLES * 2 * PAD, HD)
    w_copy.wait()
    columns_here = w_buf.shape[1]
    product = jnp.zeros((SAMPLES, columns_here), F32)
    for j in range(2 * PER):
        start = (j // PER) * PAD + j % PER
        a = mix_f[pl.ds(start, SAMPLES, stride=2 * PAD), :].astype(BF16)
        product = product + dot(a, w_buf[j * HD : (j + 1) * HD, :])
    part[...] = product

    part_copies = []
    for k in range(1, GROUPS):
        to = rem(g + k, GROUPS)
        copy = remote(part, parts.at[g], part_send.at[k - 1], part_recv.at[k - 1], (c, to))
        copy.start()
        part_copies.append(copy)
    parts[g] = product
    for copy in part_copies:
        copy.wait()
    for copy in kv_copies:
        copy.wait_send()
    decode_out[...] = (parts[0] + parts[1]) + (parts[2] + parts[3])


def span_kernel(
    limit_ref, q_ref, span_ref, prefix_ref,
    out_ref,
    kv, kp, vp, acc, top,
    send, recv,
):
    c = lax.axis_index("ctx")
    g = lax.axis_index("kvh")
    limit = limit_ref[0]
    z, x, y = c // 8, rem(c // 2, 4), rem(c, 2)

    def at(z_, x_, y_):
        return z_ * 8 + x_ * 2 + y_

    along_z = ((at(rem(z + 1, 4), x, y), g), (at(rem(z + 3, 4), x, y), g))
    along_x = ((at(z, rem(x + 1, 4), y), g), (at(z, rem(x + 3, 4), y), g))
    along_y = (at(z, x, 1 - y), g)
    minor = (along_x, along_z)
    major = (along_z, along_x)

    for h in range(2):
        cols = slice(h * HD, (h + 1) * HD)
        kv[h, 0, :, :SPAN_ROWS, :] = span_ref[:, :, cols]
        kv[h, 0, :, SPAN_ROWS:, :] = prefix_ref[:, :, cols]

    greet((along_z[0], along_z[1], along_x[0], along_x[1], along_y))

    sent = [0, 0]
    copies = []

    def give(h, src, dst, device):
        copy = remote(kv.at[h, src], kv.at[h, dst], send.at[h, sent[h]], recv.at[h, dst], device)
        sent[h] += 1
        copy.start()
        copies.append(copy)

    def take(h, slot):
        remote(kv.at[h, slot], kv.at[h, slot], send.at[h, 0], recv.at[h, slot], along_y).wait_recv()

    def slot(big, small, last):
        return big * 8 + small * 2 + last

    def both(h, axis, src, dst_next, dst_previous):
        give(h, src, dst_next, axis[h][0])
        give(h, src, dst_previous, axis[h][1])

    def big_step(h, small, last):
        both(h, major, slot(0, small, last), slot(3, small, last), slot(1, small, last))

    for h in range(2):
        give(h, 0, slot(0, 0, 1), along_y)
    for h in range(2):
        both(h, minor, slot(0, 0, 0), slot(0, 3, 0), slot(0, 1, 0))
    for h in range(2):
        big_step(h, 0, 0)

    row = lax.broadcasted_iota(jnp.int32, (SPAN_ROWS, SPAN_ROWS), 0)
    col = lax.broadcasted_iota(jnp.int32, (SPAN_ROWS, SPAN_ROWS), 1)
    causal = col <= row
    ones = jnp.ones((SPAN_ROWS, HD), BF16)

    def query(j):
        return q_ref[:, pl.ds(pl.multiple_of(j * HD, HD), HD)]

    for h in range(2):
        key = kv[h, 0, 0, :SPAN_ROWS, :]
        value = jnp.concatenate([kv[h, 0, 1, :SPAN_ROWS, :], ones], axis=1)

        def first(j, carry, h=h, key=key, value=value):
            s = jnp.where(causal, dot_t(query(h * PER + j), key) * SCALE, MASKED)
            highest = jnp.max(s, axis=1, keepdims=True)
            weights = jnp.exp2(s - highest).astype(BF16)
            acc[h * PER + j] = dot(weights, value)
            top[h * PER + j] = jnp.broadcast_to(highest, (SPAN_ROWS, HD))
            return carry

        lax.fori_loop(0, PER, first, 0)

    for h in range(2):
        take(h, slot(0, 0, 1))
    for h in range(2):
        both(h, minor, slot(0, 0, 1), slot(0, 3, 1), slot(0, 1, 1))
    for h in range(2):
        big_step(h, 0, 1)
    for h in range(2):
        take(h, slot(0, 3, 0))
        give(h, slot(0, 3, 0), slot(0, 2, 0), minor[h][0])
        take(h, slot(0, 1, 0))
        take(h, slot(0, 1, 1))
        give(h, slot(0, 1, 1), slot(0, 2, 1), minor[h][1])
        take(h, slot(0, 3, 1))
    for h in range(2):
        big_step(h, 3, 0)
        big_step(h, 1, 0)
    for h in range(2):
        big_step(h, 3, 1)
        big_step(h, 1, 1)
    for h in range(2):
        take(h, slot(0, 2, 0))
        take(h, slot(0, 2, 1))
    for h in range(2):
        big_step(h, 2, 0)
        big_step(h, 2, 1)

    pre_row = lax.broadcasted_iota(jnp.int32, (PRE_ROWS, HD), 0)
    one = jnp.ones((SPAN_ROWS, HD), F32)

    def chunk(h, slots):
        sub = kv[h, 0, 0, 0:1, :].astype(F32)
        for n, (big, small, last) in enumerate(slots):
            s = slot(big, small, last)
            dz, dx = (big, small) if h == 0 else (small, big)
            from_c = at(rem(z + dz, 4), rem(x + dx, 4), y if last == 0 else 1 - y)
            span_ok = jnp.full((SPAN_ROWS, HD), from_c, jnp.int32) < c
            pre_ok = from_c * PRE_ROWS + pre_row < limit
            here = n * ROWS
            kp[here : here + SPAN_ROWS, :] = jnp.where(
                span_ok, kv[h, s, 0, :SPAN_ROWS, :].astype(F32), sub
            ).astype(BF16)
            vp[here : here + SPAN_ROWS, :HD] = jnp.where(
                span_ok, kv[h, s, 1, :SPAN_ROWS, :].astype(F32), 0.0
            ).astype(BF16)
            vp[here : here + SPAN_ROWS, HD:] = jnp.where(span_ok, one, 0.0).astype(BF16)
            there = here + SPAN_ROWS
            kp[there : there + PRE_ROWS, :] = jnp.where(
                pre_ok, kv[h, s, 0, SPAN_ROWS:, :].astype(F32), sub
            ).astype(BF16)
            vp[there : there + PRE_ROWS, :HD] = jnp.where(
                pre_ok, kv[h, s, 1, SPAN_ROWS:, :].astype(F32), 0.0
            ).astype(BF16)
            vp[there : there + PRE_ROWS, HD:] = jnp.where(pre_ok, 1.0, 0.0).astype(BF16)

        def step(j, carry):
            head = h * PER + j
            s = dot_t(query(head), kp[...]) * SCALE
            before = top[head]
            highest = jnp.maximum(before, jnp.max(s, axis=1, keepdims=True))
            weights = jnp.exp2(s - highest[:, :1]).astype(BF16)
            rescale = jnp.exp2(before - highest)
            acc[head] = acc[head] * jnp.concatenate([rescale, rescale], axis=1) + dot(weights, vp[...])
            top[head] = highest
            return carry

        lax.fori_loop(0, PER, step, 0)

    halves = (
        ((0, 0), (0, 1), (3, 0), (1, 0)),
        ((3, 1), (1, 1), (2, 0), (2, 1)),
    )

    def blocks(big, half):
        return [(big, small, last) for small, last in halves[half]]

    for half in range(2):
        for h in range(2):
            chunk(h, blocks(0, half))
    for half in range(2):
        for big in (3, 1):
            for h in range(2):
                for small, last in halves[half]:
                    take(h, slot(big, small, last))
                    if last == (0 if big == 3 else 1):
                        give(h, slot(big, small, last), slot(2, small, last), major[h][0 if big == 3 else 1])
        for big in (3, 1):
            for h in range(2):
                chunk(h, blocks(big, half))
    for half in range(2):
        for h in range(2):
            for small, last in halves[half]:
                take(h, slot(2, small, last))
            chunk(h, blocks(2, half))

    def finish(j, carry):
        out_ref[:, pl.ds(pl.multiple_of(j * HD, HD), HD)] = acc[j, :, :HD] / acc[j, :, HD:]
        return carry

    lax.fori_loop(0, 2 * PER, finish, 0)
    for copy in copies:
        copy.wait_send()


def shards(
    span_queries,
    span_keyvals,
    prefix_keyvals,
    offset,
    decode_queries,
    private_keyvals,
    suffix_lengths,
    out_weight,
):
    vmem = pl.BlockSpec(memory_space=pltpu.VMEM)
    smem = pl.BlockSpec(memory_space=pltpu.SMEM)
    hbm = pl.BlockSpec(memory_space=pl.ANY)
    dma = pltpu.SemaphoreType.DMA
    group = 2 * PER * HD
    wide = out_weight.shape[1]
    private = private_keyvals.reshape(2, SAMPLES * 8, KVH * HD)
    limit_bytes = 60 * 1024 * 1024
    prefix_group, relaid_span, decode_output = pl.pallas_call(
        decode_kernel,
        out_shape=(
            jax.ShapeDtypeStruct((2, PRE_ROWS, 2 * HD), BF16),
            jax.ShapeDtypeStruct((2, SPAN_ROWS // GROUPS, KVH * HD), BF16),
            jax.ShapeDtypeStruct((SAMPLES, wide), F32),
        ),
        in_specs=[smem, smem, vmem, vmem, vmem, hbm, hbm],
        out_specs=(vmem, vmem, vmem),
        scratch_shapes=[
            pltpu.VMEM((group, wide), BF16),
            pltpu.VMEM((SAMPLES, group), BF16),
            pltpu.VMEM((2 * SAMPLES * PAD, HD), F32),
            pltpu.VMEM((GROUPS, 2, SAMPLES * 8, 2 * HD), BF16),
            pltpu.VMEM((SAMPLES * 8, HD), jnp.int32),
            pltpu.VMEM((SAMPLES, 3, PAD, HD), BF16),
            pltpu.VMEM((CTX, 3, PAD, HD), BF16),
            pltpu.VMEM((2, PAD, HD), BF16),
            pltpu.VMEM((CTX, 2, PAD, HD), BF16),
            pltpu.VMEM((SAMPLES * 2 * PAD, HD), F32),
            pltpu.VMEM((SAMPLES, wide), F32),
            pltpu.VMEM((GROUPS, SAMPLES, wide), F32),
            dma, dma, dma((3, GROUPS - 1)), dma((3, GROUPS - 1)), dma((3,)),
            dma((CTX,)), dma((CTX,)), dma((CTX,)), dma((CTX,)), dma((GROUPS - 1,)), dma((GROUPS - 1,)),
        ],
        compiler_params=pltpu.CompilerParams(
            collective_id=0, has_side_effects=True, vmem_limit_bytes=limit_bytes
        ),
        name="decode",
    )(offset, suffix_lengths, span_keyvals, prefix_keyvals, private, decode_queries, out_weight)
    span_attention = pl.pallas_call(
        span_kernel,
        out_shape=jax.ShapeDtypeStruct((SPAN_ROWS, group), F32),
        in_specs=[smem, vmem, vmem, vmem],
        out_specs=vmem,
        scratch_shapes=[
            pltpu.VMEM((2, CTX, 2, ROWS, HD), BF16),
            pltpu.VMEM((4 * ROWS, HD), BF16),
            pltpu.VMEM((4 * ROWS, 2 * HD), BF16),
            pltpu.VMEM((2 * PER, SPAN_ROWS, 2 * HD), F32),
            pltpu.VMEM((2 * PER, SPAN_ROWS, HD), F32),
            dma((2, CTX)), dma((2, CTX)),
        ],
        compiler_params=pltpu.CompilerParams(
            collective_id=1, has_side_effects=True, vmem_limit_bytes=limit_bytes
        ),
        name="span",
    )(offset, span_queries, span_keyvals, prefix_group)
    return (span_attention, relaid_span, decode_output)


def solution(mesh):
    return jax.shard_map(
        shards,
        mesh=mesh,
        in_specs=(
            P("ctx", "kvh"),
            P(None, "ctx", "kvh"),
            P(None, ("ctx", "kvh"), None),
            P(),
            P(),
            P(None, None, ("ctx", "kvh"), None),
            P(),
            P("kvh", "ctx"),
        ),
        out_specs=(P("ctx", "kvh"), P(None, ("ctx", "kvh"), None), P(None, "ctx")),
        check_vma=False,
    )
```

time: 850 us -> 201 us (0.24)
  waiting for transfers between devices: 415 us -> 0 us
  blocking collectives: 249 us -> 0 us
  Pallas kernels: 0 us -> 196 us
  local copies, waits for them, and re-layouts: 67.3 us -> 4.02 us
  matrix products: 58.1 us -> 0 us
  other arithmetic: 37.4 us -> 0 us
  between operations: 14.7 us -> 1.31 us
    all_gather x2 -> x0, waiting for transfers between devices: 232 us -> none  [the longest x1 136 us: shards(): group_prefix = lax.all_gather(relaid, 'ctx', axis=1, tiled=True)]
    pallas_call x0 -> x2, Pallas kernels: none -> 196 us  [the longest x1 149 us: shards(): pl.pallas_call(span_kernel, out_shape=jax.ShapeDtypeStruct((SPAN_ROWS, gr...]
    psum x2 -> x0, blocking collectives: 171 us -> none  [the longest x1 157 us: shards(): own_sum, own_total = lax.psum((share_sum, share_total), 'ctx')]
    psum x1 -> x0, waiting for transfers between devices: 138 us -> none  [shards(): own_sum, own_total = lax.psum((share_sum, share_total), 'ctx')]
    pmax x1 -> x0, blocking collectives: 69.1 us -> none  [shards(): highest = lax.pmax(sample_max, ('ctx', 'kvh'))]
    dot_general x29 -> x0, matrix products: 58.1 us -> none  [the longest x12 32.7 us: fold_block(): jnp.einsum('hgqk,khd->qhgd', weights, values, preferred_element_type=jnp....]
    reduce_scatter x1 -> x0, waiting for transfers between devices: 30.7 us -> none  [shards(): lax.psum_scatter(scaled, 'kvh', scatter_dimension=1, tiled=True)]
    reduce_sum x13 -> x0, other arithmetic: 26.8 us -> none  [the longest x12 25.3 us: fold_block(): totals = totals * rescale + jnp.sum(weights.astype(jnp.float32), axis=-1)]
  transfers between devices with their start and end apart: 6 -> 0, of which waited for: 5 -> 0; matrix products, arithmetic and copies ran while one was open for 9% -> 0% of each run, Pallas kernels for 0% -> 0%
where the time goes in v1:
time: 201 us
  Pallas kernels  196 us (98%)
  local copies, waits for them, and re-layouts  4.02 us (2%)
    pallas_call x1, Pallas kernels, shards(): pl.pallas_call(span_kernel, out_shape=jax.ShapeDtypeStruct((SPAN_ROWS, gr...  149 us
    pallas_call x1, Pallas kernels, shards(): pl.pallas_call(decode_kernel, out_shape=(jax.ShapeDtypeStruct((2, PRE_ROW...  46.6 us

profile of v1, /device:TPU:0, one launch (start us, length us, event | category | flops | bytes accessed | tf_op | source)
XLA Modules:
  0.0 201.0 jit_solution(569663516268308282)
XLA Ops:
  1.3 46.6 %decode.1 = (bf16[2,64,256]{2,1,0:T(8,128)(2,1)}, bf16[2,32,1024]{2,1,0:T(8,128)(2,1)}, f32[32,384]{1,0:T(8,128)}) custom-call(s32[1]{0:T(128)S(6)} %copy.14.limit_ref, s32[32]{0:T(128)} %suffix_ref.1, bf16[2,128,256]{2,1,0:T(8,128)(2,1)} %span_ref.3, bf16[2,16,1024]{2,1,0:T(8,128)(2,1)} %prefix_ref.1, bf16[2,256,1024]{2,1,0:T(8,128)(2,1)} %bitcast.1, ...), custom_call_target="tpu_custom_call" | custom-call | tf_op jit(solution)/shard_map/decode/pallas_call | solution.py:457
  47.8 149.2 %span.1 = f32[128,3072]{1,0:T(8,128)} custom-call(s32[1]{0:T(128)S(6)} %copy.14.limit_ref, bf16[128,3072]{1,0:T(8,128)(2,1)} %q_ref.1, bf16[2,128,256]{2,1,0:T(8,128)(2,1)} %span_ref.3, bf16[2,64,256]{2,1,0:T(8,128)(2,1)} %get-tuple-element.6.prefix_ref), custom_call_target="tpu_custom_call" | custom-call | tf_op jit(solution)/shard_map/span/pallas_call | solution.py:487
  197.0 0.0 copy-start
  197.0 0.0 copy-start.1
  197.0 2.7 %copy.15 = f32[128,3072]{1,0:T(8,128)} copy(f32[128,3072]{1,0:T(8,128)} %span.1) | data formatting | bytes 3145728
  199.8 0.0 copy-done
  199.8 0.7 copy.16
  200.4 0.0 copy-done.1
  200.4 0.6 copy.17
Async XLA Ops:
  197.0 2.8 %copy-start = (bf16[2,32,1024]{2,1,0:T(8,128)(2,1)S(1)}, bf16[2,32,1024]{2,1,0:T(8,128)(2,1)}, u32[]{:S(2)}) copy-start(bf16[2,32,1024]{2,1,0:T(8,128)(2,1)} %get-tuple-element.13) | copy-start | bytes 393220
  197.0 3.4 %copy-start.1 = (f32[32,384]{1,0:T(8,128)S(1)}, f32[32,384]{1,0:T(8,128)}, u32[]{:S(2)}) copy-start(f32[32,384]{1,0:T(8,128)} %get-tuple-element.14) | copy-start | bytes 147460

commit v2 on v0

v2 whole, which is shorter than its diff:
```python
import jax
import jax.numpy as jnp
from jax import lax
from jax.experimental import pallas as pl
from jax.experimental.pallas import tpu as pltpu
from jax.sharding import PartitionSpec as P

H = 96
KVH = 8
HD = 128
CTX = 32
GROUPS = 4
SAMPLES = 32
PER = H // KVH
PAD = 16
SPAN_ROWS = 128
PRE_ROWS = 64
ROWS = SPAN_ROWS + PRE_ROWS
PREFIX = 2048
LOG2E = 1.4426950408889634
SCALE = HD ** (-0.5) * LOG2E
MASKED = -1e30
TILE = 512
TILES = 2 * PER * SPAN_ROWS // TILE
CHUNK = 8 * ROWS

MESH = pl.DeviceIdType.MESH
F32 = jnp.float32
BF16 = jnp.bfloat16


def rem(a, n):
    return lax.rem(a, jnp.int32(n))


def dot_t(a, b):
    return lax.dot_general(a, b, (((1,), (1,)), ((), ())), preferred_element_type=F32)


def dot(a, b):
    return jnp.dot(a, b, preferred_element_type=F32)


def remote(src, dst, send, recv, device):
    return pltpu.make_async_remote_copy(
        src_ref=src, dst_ref=dst, send_sem=send, recv_sem=recv, device_id=device, device_id_type=MESH
    )


def kernel(
    limit_ref, suffix_ref, q_ref, span_ref, prefix_ref, private_ref, dq_ref, w_ref,
    out_ref, relaid_out, decode_out,
    kv, kp, vp, acc, top, scores, tops, qs, prefix_group,
    w_buf, dq_buf, qf, priv, suf, msg, inbox, mix_own, mix_all, mix_f, part, parts,
    send, recv, recv_own, local, kv_send, kv_recv, own_sem,
    in_send, in_recv, mix_send, mix_recv, part_send, part_recv,
):
    c = lax.axis_index("ctx")
    g = lax.axis_index("kvh")
    limit = limit_ref[0]
    z, x, y = c // 8, rem(c // 2, 4), rem(c, 2)
    width = 2 * HD

    w_copy = pltpu.make_async_copy(w_ref, w_buf, local.at[0])
    w_copy.start()
    dq_copy = pltpu.make_async_copy(
        dq_ref.at[:, pl.ds(pl.multiple_of(g * 2 * PER * HD, HD), 2 * PER * HD)], dq_buf, local.at[1]
    )
    dq_copy.start()
    for j in range(2 * PER):
        pltpu.make_async_copy(
            q_ref.at[:, j * HD : (j + 1) * HD], qs.at[j * SPAN_ROWS : (j + 1) * SPAN_ROWS, :], local.at[2]
        ).start()

    barrier = pltpu.get_barrier_semaphore()
    for k in range(1, GROUPS):
        pl.semaphore_signal(barrier, inc=1, device_id=(c, rem(g + k, GROUPS)), device_id_type=MESH)

    def greet_ctx(k, carry):
        pl.semaphore_signal(barrier, inc=1, device_id=(rem(c + k, CTX), g), device_id_type=MESH)
        return carry

    lax.fori_loop(1, CTX, greet_ctx, 0)
    pl.semaphore_wait(barrier, CTX - 1 + GROUPS - 1)

    def at(z_, x_, y_):
        return z_ * 8 + x_ * 2 + y_

    along_z = ((at(rem(z + 1, 4), x, y), g), (at(rem(z + 3, 4), x, y), g))
    along_x = ((at(z, rem(x + 1, 4), y), g), (at(z, rem(x + 3, 4), y), g))
    along_y = (at(z, x, 1 - y), g)
    minor = (along_x, along_z)
    major = (along_z, along_x)
    sent = [0, 0]
    copies = []

    def slot(big, small, last):
        return big * 8 + small * 2 + last

    def give(h, src, dst, device, sem):
        copy = remote(src, dst, send.at[h, sent[h]], sem, device)
        sent[h] += 1
        copy.start()
        copies.append(copy)

    def give_block(h, src, dst, device):
        give(h, kv.at[h, src], kv.at[h, dst], device, recv.at[h, dst])

    own_targets = [
        (slot(0, 0, 1), lambda h: along_y),
        (slot(0, 3, 0), lambda h: minor[h][0]),
        (slot(0, 1, 0), lambda h: minor[h][1]),
        (slot(3, 0, 0), lambda h: major[h][0]),
        (slot(1, 0, 0), lambda h: major[h][1]),
    ]
    own_slots = [dst for dst, _ in own_targets]

    def take(h, s):
        if s in own_slots:
            n = own_slots.index(s)
            first = kv.at[h, s, :, :SPAN_ROWS, :]
            second = kv.at[h, s, :, SPAN_ROWS:, :]
            remote(first, first, send.at[h, 0], recv_own.at[h, n], along_y).wait_recv()
            remote(second, second, send.at[h, 0], recv.at[h, s], along_y).wait_recv()
        else:
            remote(kv.at[h, s], kv.at[h, s], send.at[h, 0], recv.at[h, s], along_y).wait_recv()

    def both(h, axis, src, dst_next, dst_previous):
        give_block(h, src, dst_next, axis[h][0])
        give_block(h, src, dst_previous, axis[h][1])

    def big_step(h, small, last):
        both(h, major, slot(0, small, last), slot(3, small, last), slot(1, small, last))

    for n, (dst, device) in enumerate(own_targets):
        for h in range(2):
            give(
                h, span_ref.at[:, :, h * HD : (h + 1) * HD], kv.at[h, dst, :, :SPAN_ROWS, :],
                device(h), recv_own.at[h, n],
            )

    def columns(which):
        return pl.ds(pl.multiple_of(which * width, width), width)

    def rows_of(which, count):
        return pl.ds(pl.multiple_of(which * count, count), count)

    kv_copies = {}

    def exchange(n, pair):
        for k in range(1, GROUPS):
            to = rem(g + k, GROUPS)
            src, dst = pair(to)
            copy = remote(src, dst, kv_send.at[n, k - 1], kv_recv.at[n, k - 1], (c, to))
            copy.start()
            kv_copies[n, k] = copy
        src, dst = pair(g)
        copy = pltpu.make_async_copy(src, dst, own_sem.at[n])
        copy.start()
        kv_copies[n, 0] = copy

    def received(n):
        kv_copies[n, 0].wait()
        for k in range(1, GROUPS):
            kv_copies[n, k].wait_recv()

    exchange(0, lambda to: (prefix_ref.at[:, :, columns(to)], prefix_group.at[:, rows_of(g, 16), :]))
    exchange(1, lambda to: (span_ref.at[:, rows_of(to, 32), :], relaid_out.at[:, :, columns(g)]))

    pltpu.make_async_copy(qs, qs, local.at[2]).wait()
    row = lax.broadcasted_iota(jnp.int32, (SPAN_ROWS, SPAN_ROWS), 0)
    col = lax.broadcasted_iota(jnp.int32, (SPAN_ROWS, SPAN_ROWS), 1)
    allowed = jnp.concatenate([col <= row] * (TILE // SPAN_ROWS), axis=0)
    ones = jnp.ones((SPAN_ROWS, HD), BF16)
    for h in range(2):
        cols = slice(h * HD, (h + 1) * HD)
        kv[h, 0, :, :SPAN_ROWS, :] = span_ref[:, :, cols]

    def tile_rows(t):
        return pl.ds(pl.multiple_of(t * TILE, TILE), TILE)

    def first(t, carry):
        h = t // (TILES // 2)
        s = jnp.where(allowed, dot_t(qs[tile_rows(t), :], kv[h, 0, 0, :SPAN_ROWS, :]) * SCALE, MASKED)
        highest = jnp.broadcast_to(jnp.max(s, axis=1, keepdims=True), (TILE, HD))
        weights = jnp.exp2(s - highest).astype(BF16)
        acc[t] = dot(weights, jnp.concatenate([kv[h, 0, 1, :SPAN_ROWS, :], ones], axis=1))
        top[t] = highest
        return carry

    lax.fori_loop(0, TILES, first, 0)

    received(0)
    for h in range(2):
        cols = slice(h * HD, (h + 1) * HD)
        kv[h, 0, :, SPAN_ROWS:, :] = prefix_group[:, :, cols]
    for n, (dst, device) in enumerate(own_targets):
        for h in range(2):
            give(
                h, kv.at[h, 0, :, SPAN_ROWS:, :], kv.at[h, dst, :, SPAN_ROWS:, :], device(h), recv.at[h, dst]
            )
    for h in range(2):
        take(h, slot(0, 0, 1))
        both(h, minor, slot(0, 0, 1), slot(0, 3, 1), slot(0, 1, 1))
        big_step(h, 0, 1)
    exchange(2, lambda to: (private_ref.at[:, :, columns(to)], priv.at[g]))

    qf[...] = jnp.zeros_like(qf)
    dq_copy.wait()
    for j in range(2 * PER):
        start = (j // PER) * SAMPLES * PAD + j % PER
        qf[pl.ds(start, SAMPLES, stride=PAD), :] = dq_buf[:, j * HD : (j + 1) * HD].astype(F32)

    def set_suffix(b, carry):
        suf[pl.ds(pl.multiple_of(b * 8, 8), 8), :] = jnp.full((8, HD), suffix_ref[b], jnp.int32)
        return carry

    lax.fori_loop(0, SAMPLES, set_suffix, 0)

    for h in range(2):
        take(h, slot(0, 3, 0))
        give_block(h, slot(0, 3, 0), slot(0, 2, 0), minor[h][0])
        take(h, slot(0, 1, 0))
        take(h, slot(0, 1, 1))
        give_block(h, slot(0, 1, 1), slot(0, 2, 1), minor[h][1])
        take(h, slot(0, 3, 1))
    for h in range(2):
        big_step(h, 3, 0)
        big_step(h, 1, 0)
    for h in range(2):
        big_step(h, 3, 1)
        big_step(h, 1, 1)
    for h in range(2):
        take(h, slot(0, 2, 0))
        take(h, slot(0, 2, 1))
    for h in range(2):
        big_step(h, 2, 0)
        big_step(h, 2, 1)

    pre_row = lax.broadcasted_iota(jnp.int32, (PRE_ROWS, HD), 0)

    def put(h, here, count, ok, key, value, sub):
        kp[h, here : here + count, :] = jnp.where(ok, key.astype(F32), sub).astype(BF16)
        vp[h, here : here + count, :HD] = jnp.where(ok, value.astype(F32), 0.0).astype(BF16)
        vp[h, here : here + count, HD:] = jnp.where(ok, 1.0, 0.0).astype(BF16)

    def score(t, n, half):
        h = t // (TILES // 2)
        q = qs[tile_rows(t), :]
        most = None
        for a in range(0, n, 2 * HD):
            s = dot_t(q, kp[h, a : a + 2 * HD, :])
            scores[half, :, a : a + 2 * HD] = s
            here = jnp.maximum(s[:, :HD], s[:, HD:])
            most = here if most is None else jnp.maximum(most, here)
        tops[half] = most

    def weigh(t, n, half):
        h = t // (TILES // 2)
        before = top[t]
        highest = jnp.maximum(
            before, jnp.broadcast_to(jnp.max(tops[half], axis=1, keepdims=True) * SCALE, (TILE, HD))
        )
        rescale = jnp.exp2(before - highest)
        top[t] = highest
        weights = jnp.concatenate(
            [
                jnp.exp2(scores[half, :, a : a + HD] * SCALE - highest).astype(BF16)
                for a in range(0, n, HD)
            ],
            axis=1,
        )
        acc[t] = acc[t] * jnp.concatenate([rescale, rescale], axis=1) + dot(weights, vp[h, :n, :])

    def chunk(blocks):
        size = len(blocks) * ROWS
        for h in range(2):
            sub = kv[h, 0, 0, 0:1, :].astype(F32)
            for n, (big, small, last) in enumerate(blocks):
                s = slot(big, small, last)
                dz, dx = (big, small) if h == 0 else (small, big)
                from_c = at(rem(z + dz, 4), rem(x + dx, 4), y if last == 0 else 1 - y)
                span_ok = jnp.full((SPAN_ROWS, HD), from_c, jnp.int32) < c
                pre_ok = from_c * PRE_ROWS + pre_row < limit
                here = n * ROWS
                put(h, here, SPAN_ROWS, span_ok, kv[h, s, 0, :SPAN_ROWS, :], kv[h, s, 1, :SPAN_ROWS, :], sub)
                put(
                    h, here + SPAN_ROWS, PRE_ROWS, pre_ok, kv[h, s, 0, SPAN_ROWS:, :], kv[h, s, 1, SPAN_ROWS:, :], sub
                )
        score(0, size, 0)

        def two(i, carry):
            score(2 * i + 1, size, 1)
            weigh(2 * i, size, 0)
            score(2 * i + 2, size, 0)
            weigh(2 * i + 1, size, 1)
            return carry

        lax.fori_loop(0, TILES // 2 - 1, two, 0)
        score(TILES - 1, size, 1)
        weigh(TILES - 2, size, 0)
        weigh(TILES - 1, size, 1)

    halves = (
        ((0, 0), (0, 1), (3, 0), (1, 0)),
        ((3, 1), (1, 1), (2, 0), (2, 1)),
    )

    def pass_on(half):
        for small, last in halves[half]:
            for h in range(2):
                for big in (3, 1):
                    take(h, slot(big, small, last))
                    if last == (0 if big == 3 else 1):
                        give_block(
                            h, slot(big, small, last), slot(2, small, last), major[h][0 if big == 3 else 1]
                        )

    chunk([(0, small, last) for half in halves for small, last in half])
    pass_on(0)

    received(2)
    pre_pos = c * PRE_ROWS + pre_row
    row_in = lax.broadcasted_iota(jnp.int32, (8 * SAMPLES, HD), 0)
    always = jnp.full((SPAN_ROWS, HD), True)
    total = ROWS + GROUPS * 8 * SAMPLES
    rows = SAMPLES * PAD
    for h in range(2):
        cols = slice(h * HD, (h + 1) * HD)
        sub = span_ref[0, 0:1, cols].astype(F32)
        kp[h, :SPAN_ROWS, :] = span_ref[0, :, cols]
        vp[h, :SPAN_ROWS, :HD] = span_ref[1, :, cols]
        vp[h, :SPAN_ROWS, HD:] = ones
        put(h, SPAN_ROWS, PRE_ROWS, pre_pos < limit, prefix_group[0, :, cols], prefix_group[1, :, cols], sub)
        for s in range(GROUPS):
            ok = (c * GROUPS + s) * 8 + (row_in & 7) < suf[...]
            put(h, ROWS + s * 8 * SAMPLES, 8 * SAMPLES, ok, priv[s, 0, :, cols], priv[s, 1, :, cols], sub)
    lane = lax.broadcasted_iota(jnp.int32, (rows, HD), 1)
    own_sample = lax.broadcasted_iota(jnp.int32, (rows, HD), 0) >> 4
    stats = jnp.zeros((rows, HD), F32)
    for h in range(2):
        q = qf[h * rows : (h + 1) * rows, :].astype(BF16)
        most = None
        spans = [(0, ROWS, False)] + [(ROWS + s * 256, 256, True) for s in range(GROUPS)]
        for start, count, masked in spans:
            s = dot_t(q, kp[h, start : start + count, :]) * SCALE
            if masked:
                key_sample = lax.broadcasted_iota(jnp.int32, (rows, count), 1) >> 3
                query_sample = lax.broadcasted_iota(jnp.int32, (rows, count), 0) >> 4
                s = jnp.where(key_sample == query_sample, s, MASKED)
            scores[h, :, start : start + count] = s
            here = jnp.max(s, axis=1, keepdims=True)
            most = here if most is None else jnp.maximum(most, here)
        weights = jnp.exp2(scores[h, :, :total] - most).astype(BF16)
        both_sums = dot(weights, vp[h, :total, :])
        total_here = both_sums[:, HD:]
        msg[:, h, :, :] = (both_sums[:, :HD] / total_here).astype(BF16).reshape(SAMPLES, PAD, HD)
        lse = most + jnp.log2(total_here)
        high = lse.astype(BF16).astype(F32)
        middle = (lse - high).astype(BF16).astype(F32)
        low = lse - high - middle
        stats = jnp.where(lane == 3 * h, high, stats)
        stats = jnp.where(lane == 3 * h + 1, middle, stats)
        stats = jnp.where(lane == 3 * h + 2, low, stats)
    msg[:, 2, :, :] = stats.astype(BF16).reshape(SAMPLES, PAD, HD)

    def in_copy(k):
        to = rem(c + k, CTX)
        return remote(msg.at[to], inbox.at[k], in_send.at[k], in_recv.at[k], (to, g))

    def mix_copy(k):
        to = rem(c + k, CTX)
        return remote(mix_own, mix_all.at[c], mix_send.at[k], mix_recv.at[k], (to, g))

    def start_in(k, carry):
        in_copy(k).start()
        return carry

    def wait_in(k, carry):
        in_copy(k).wait()
        return carry

    def start_mix(k, carry):
        mix_copy(k).start()
        return carry

    def wait_mix(k, carry):
        mix_copy(k).wait()
        return carry

    lax.fori_loop(1, CTX, start_in, 0)
    inbox[0] = msg[c]

    chunk([(big, small, last) for big in (3, 1) for small, last in halves[0]])
    pass_on(1)

    lax.fori_loop(1, CTX, wait_in, 0)
    stat = inbox[:, 2, :, :].astype(F32)
    for h in range(2):
        lse = stat[:, :, 3 * h : 3 * h + 1] + stat[:, :, 3 * h + 1 : 3 * h + 2] + stat[:, :, 3 * h + 2 : 3 * h + 3]
        weight = jnp.exp2(lse - jnp.max(lse, axis=0, keepdims=True))
        mixed = jnp.sum(weight * inbox[:, h, :, :].astype(F32), axis=0) / jnp.sum(weight, axis=0)
        mix_own[h] = mixed.astype(BF16)
    lax.fori_loop(1, CTX, start_mix, 0)
    mix_all[c] = mix_own[...]

    chunk([(big, small, last) for big in (3, 1) for small, last in halves[1]])

    lax.fori_loop(1, CTX, wait_mix, 0)
    mix_f[...] = mix_all[...].astype(F32).reshape(SAMPLES * 2 * PAD, HD)
    w_copy.wait()
    columns_here = w_buf.shape[1]
    product = jnp.zeros((SAMPLES, columns_here), F32)
    for j in range(2 * PER):
        start = (j // PER) * PAD + j % PER
        a = mix_f[pl.ds(start, SAMPLES, stride=2 * PAD), :].astype(BF16)
        product = product + dot(a, w_buf[j * HD : (j + 1) * HD, :])
    part[...] = product
    part_copies = []
    for k in range(1, GROUPS):
        to = rem(g + k, GROUPS)
        copy = remote(part, parts.at[g], part_send.at[k - 1], part_recv.at[k - 1], (c, to))
        copy.start()
        part_copies.append(copy)
    parts[g] = product

    for half in range(2):
        for small, last in halves[half]:
            for h in range(2):
                take(h, slot(2, small, last))
        chunk([(2, small, last) for small, last in halves[half]])

    for j in range(2 * PER):
        t, r = j * SPAN_ROWS // TILE, j * SPAN_ROWS % TILE
        here = slice(r, r + SPAN_ROWS)
        out_ref[:, j * HD : (j + 1) * HD] = acc[t, here, :HD] / acc[t, here, HD:]

    for copy in part_copies:
        copy.wait()
    decode_out[...] = (parts[0] + parts[1]) + (parts[2] + parts[3])
    received(1)
    for (n, k), copy in kv_copies.items():
        if k:
            copy.wait_send()
    for copy in copies:
        copy.wait_send()


def shards(
    span_queries,
    span_keyvals,
    prefix_keyvals,
    offset,
    decode_queries,
    private_keyvals,
    suffix_lengths,
    out_weight,
):
    vmem = pl.BlockSpec(memory_space=pltpu.VMEM)
    smem = pl.BlockSpec(memory_space=pltpu.SMEM)
    hbm = pl.BlockSpec(memory_space=pl.ANY)
    dma = pltpu.SemaphoreType.DMA
    group = 2 * PER * HD
    wide = out_weight.shape[1]
    private = private_keyvals.reshape(2, SAMPLES * 8, KVH * HD)
    return pl.pallas_call(
        kernel,
        out_shape=(
            jax.ShapeDtypeStruct((SPAN_ROWS, group), F32),
            jax.ShapeDtypeStruct((2, SPAN_ROWS // GROUPS, KVH * HD), BF16),
            jax.ShapeDtypeStruct((SAMPLES, wide), F32),
        ),
        in_specs=[smem, smem, hbm, vmem, vmem, hbm, hbm, hbm],
        out_specs=(vmem, vmem, vmem),
        scratch_shapes=[
            pltpu.VMEM((2, CTX, 2, ROWS, HD), BF16),
            pltpu.VMEM((2, CHUNK, HD), BF16),
            pltpu.VMEM((2, CHUNK, 2 * HD), BF16),
            pltpu.VMEM((TILES, TILE, 2 * HD), F32),
            pltpu.VMEM((TILES, TILE, HD), F32),
            pltpu.VMEM((2, TILE, CHUNK), F32),
            pltpu.VMEM((2, TILE, HD), F32),
            pltpu.VMEM((group, HD), BF16),
            pltpu.VMEM((2, PRE_ROWS, 2 * HD), BF16),
            pltpu.VMEM((group, wide), BF16),
            pltpu.VMEM((SAMPLES, group), BF16),
            pltpu.VMEM((2 * SAMPLES * PAD, HD), F32),
            pltpu.VMEM((GROUPS, 2, SAMPLES * 8, 2 * HD), BF16),
            pltpu.VMEM((SAMPLES * 8, HD), jnp.int32),
            pltpu.VMEM((SAMPLES, 3, PAD, HD), BF16),
            pltpu.VMEM((CTX, 3, PAD, HD), BF16),
            pltpu.VMEM((2, PAD, HD), BF16),
            pltpu.VMEM((CTX, 2, PAD, HD), BF16),
            pltpu.VMEM((SAMPLES * 2 * PAD, HD), F32),
            pltpu.VMEM((SAMPLES, wide), F32),
            pltpu.VMEM((GROUPS, SAMPLES, wide), F32),
            dma((2, 40)), dma((2, CTX)), dma((2, 5)), dma((3,)),
            dma((3, GROUPS - 1)), dma((3, GROUPS - 1)), dma((3,)),
            dma((CTX,)), dma((CTX,)), dma((CTX,)), dma((CTX,)), dma((GROUPS - 1,)), dma((GROUPS - 1,)),
        ],
        compiler_params=pltpu.CompilerParams(
            collective_id=0, has_side_effects=True, vmem_limit_bytes=60 * 1024 * 1024
        ),
        name="attention",
    )(offset, suffix_lengths, span_queries, span_keyvals, prefix_keyvals, private, decode_queries, out_weight)


def solution(mesh):
    return jax.shard_map(
        shards,
        mesh=mesh,
        in_specs=(
            P("ctx", "kvh"),
            P(None, "ctx", "kvh"),
            P(None, ("ctx", "kvh"), None),
            P(),
            P(),
            P(None, None, ("ctx", "kvh"), None),
            P(),
            P("kvh", "ctx"),
        ),
        out_specs=(P("ctx", "kvh"), P(None, ("ctx", "kvh"), None), P(None, "ctx")),
        check_vma=False,
    )
```

time: 850 us -> 76.5 us (0.09)
  waiting for transfers between devices: 415 us -> 0 us
  blocking collectives: 249 us -> 0 us
  Pallas kernels: 0 us -> 71 us
  local copies, waits for them, and re-layouts: 67.3 us -> 4.02 us
  matrix products: 58.1 us -> 0 us
  other arithmetic: 37.4 us -> 0 us
  between operations: 14.7 us -> 1.3 us
    all_gather x2 -> x0, waiting for transfers between devices: 232 us -> none  [the longest x1 136 us: shards(): group_prefix = lax.all_gather(relaid, 'ctx', axis=1, tiled=True)]
    psum x2 -> x0, blocking collectives: 171 us -> none  [the longest x1 157 us: shards(): own_sum, own_total = lax.psum((share_sum, share_total), 'ctx')]
    psum x1 -> x0, waiting for transfers between devices: 138 us -> none  [shards(): own_sum, own_total = lax.psum((share_sum, share_total), 'ctx')]
    pallas_call x0 -> x1, Pallas kernels: none -> 71 us  [shards(): pl.pallas_call(kernel, out_shape=(jax.ShapeDtypeStruct((SPAN_ROWS, group)...]
    pmax x1 -> x0, blocking collectives: 69.1 us -> none  [shards(): highest = lax.pmax(sample_max, ('ctx', 'kvh'))]
    dot_general x29 -> x0, matrix products: 58.1 us -> none  [the longest x12 32.7 us: fold_block(): jnp.einsum('hgqk,khd->qhgd', weights, values, preferred_element_type=jnp....]
    reduce_scatter x1 -> x0, waiting for transfers between devices: 30.7 us -> none  [shards(): lax.psum_scatter(scaled, 'kvh', scatter_dimension=1, tiled=True)]
    reduce_sum x13 -> x0, other arithmetic: 26.8 us -> none  [the longest x12 25.3 us: fold_block(): totals = totals * rescale + jnp.sum(weights.astype(jnp.float32), axis=-1)]
  transfers between devices with their start and end apart: 6 -> 0, of which waited for: 5 -> 0; matrix products, arithmetic and copies ran while one was open for 9% -> 0% of each run, Pallas kernels for 0% -> 0%
where the time goes in v2:
time: 76.5 us; the launch traced here: 76.4 us
  Pallas kernels  71 us (93%)
  local copies, waits for them, and re-layouts  4.02 us (5%)
  between operations  1.3 us (2%)
    pallas_call x1, Pallas kernels, shards(): pl.pallas_call(kernel, out_shape=(jax.ShapeDtypeStruct((SPAN_ROWS, group)...  71 us
    unnamed x7, local copies, waits for them, and re-layouts  4.02 us

profile of v2, /device:TPU:0, one launch (start us, length us, event | category | flops | bytes accessed | tf_op | source)
XLA Modules:
  0.0 76.4 jit_solution(7418755230830615596)
XLA Ops:
  1.3 71.0 %attention.1 = (f32[128,3072]{1,0:T(8,128)}, bf16[2,32,1024]{2,1,0:T(8,128)(2,1)}, f32[32,384]{1,0:T(8,128)}) custom-call(s32[1]{0:T(128)S(6)} %copy.14.limit_ref, s32[32]{0:T(128)} %suffix_ref.1, bf16[128,3072]{1,0:T(8,128)(2,1)} %q_ref.1, bf16[2,128,256]{2,1,0:T(8,128)(2,1)} %span_ref.1, bf16[2,16,1024]{2,1,0:T(8,128)(2,1)} %prefix_ref.1, ...), custom_call_target="tpu_custom_call" | custom-call | tf_op jit(solution)/shard_map/attention/pallas_call | solution.py:466
  72.3 0.0 copy-start
  72.3 0.0 copy-start.1
  72.3 2.7 %copy.15 = f32[128,3072]{1,0:T(8,128)} copy(f32[128,3072]{1,0:T(8,128)} %get-tuple-element.6) | data formatting | bytes 3145728
  75.1 0.0 copy-done
  75.1 0.7 copy.16
  75.7 0.0 copy-done.1
  75.7 0.6 copy.17
Async XLA Ops:
  72.3 2.8 %copy-start = (bf16[2,32,1024]{2,1,0:T(8,128)(2,1)S(1)}, bf16[2,32,1024]{2,1,0:T(8,128)(2,1)}, u32[]{:S(2)}) copy-start(bf16[2,32,1024]{2,1,0:T(8,128)(2,1)} %get-tuple-element.7) | copy-start | bytes 393220
  72.3 3.4 %copy-start.1 = (f32[32,384]{1,0:T(8,128)S(1)}, f32[32,384]{1,0:T(8,128)}, u32[]{:S(2)}) copy-start(f32[32,384]{1,0:T(8,128)} %get-tuple-element.8) | copy-start | bytes 147460

commit v3 on v2

v3 whole, which is shorter than its diff:
```python
import jax
import jax.numpy as jnp
from jax import lax
from jax.experimental import pallas as pl
from jax.experimental.pallas import tpu as pltpu
from jax.sharding import PartitionSpec as P

H = 96
KVH = 8
HD = 128
CTX = 32
GROUPS = 4
SAMPLES = 32
PER = H // KVH
PAD = 16
SPAN_ROWS = 128
PRE_ROWS = 64
ROWS = SPAN_ROWS + PRE_ROWS
PREFIX = 2048
LOG2E = 1.4426950408889634
SCALE = HD ** (-0.5) * LOG2E
MASKED = -1e30
LEAST = 2.0**-100
TILE = 512
TILES = 2 * PER * SPAN_ROWS // TILE
CHUNK = 8 * ROWS
HALF = PER * HD
TOTAL = 2 * ROWS + GROUPS * 8 * SAMPLES
PLANE = 8
STACK = 4

MESH = pl.DeviceIdType.MESH
F32 = jnp.float32
BF16 = jnp.bfloat16


def rem(a, n):
    return lax.rem(a, jnp.int32(n))


def dot_t(a, b):
    return lax.dot_general(a, b, (((1,), (1,)), ((), ())), preferred_element_type=F32)


def dot(a, b):
    return jnp.dot(a, b, preferred_element_type=F32)


def remote(src, dst, send, recv, device):
    return pltpu.make_async_remote_copy(
        src_ref=src, dst_ref=dst, send_sem=send, recv_sem=recv, device_id=device, device_id_type=MESH
    )


def kernel(
    limit_ref, suffix_ref, q_ref, span_ref, prefix_ref, private_ref, dq_ref, w_ref,
    out_ref, relaid_out, decode_out,
    kv, kp, vp, dk, dv, acc, top, scores, tops, qs, back, back_in,
    w_buf, dq_buf, qf, priv, suf, bias, msg, inbox, mix_own, mix_all, mix_f, part, parts,
    send, recv, local, kv_send, kv_recv, own_sem, pre_send, pre_recv, pair_send, pair_recv,
    ex_send, ex_recv, part_send, part_recv,
):
    c = lax.axis_index("ctx")
    g = lax.axis_index("kvh")
    limit = limit_ref[0]
    z, x, y = c // 8, rem(c // 2, 4), rem(c, 2)
    mate = c + 1 - 2 * y
    pair = c // 2
    width = 2 * HD

    def lanes(start, size):
        return pl.ds(pl.multiple_of(start, HD), size)

    q_copy = pltpu.make_async_copy(q_ref.at[:, lanes(y * HALF, HALF)], qs.at[1], local.at[2])
    q_copy.start()
    dq_copy = pltpu.make_async_copy(dq_ref.at[:, lanes(g * 2 * HALF, 2 * HALF)], dq_buf, local.at[1])
    dq_copy.start()
    w_copy = pltpu.make_async_copy(w_ref, w_buf, local.at[0])
    w_copy.start()

    barrier = pltpu.get_barrier_semaphore()
    for k in range(1, GROUPS):
        for other in (c, mate):
            pl.semaphore_signal(barrier, inc=1, device_id=(other, rem(g + k, GROUPS)), device_id_type=MESH)

    def greet_ctx(k, carry):
        pl.semaphore_signal(barrier, inc=1, device_id=(rem(c + k, CTX), g), device_id_type=MESH)
        return carry

    lax.fori_loop(1, CTX, greet_ctx, 0)
    mine = jnp.where(y == 0, span_ref[:, :, :HD], span_ref[:, :, HD:])
    kv[y, 0, :, :SPAN_ROWS, :] = mine
    pl.semaphore_wait(barrier, 2 * (GROUPS - 1) + CTX - 1)

    along_y = (mate, g)
    span_copy = remote(
        span_ref.at[:, :, lanes((1 - y) * HD, HD)], kv.at[y, 0, :, :SPAN_ROWS, :],
        pair_send.at[0], pair_recv.at[0], along_y,
    )
    span_copy.start()
    pre_copies = []
    for dy, other_y, other_c in ((1, 1 - y, mate), (0, y, c)):
        for k in range(GROUPS):
            to = rem(g + k, GROUPS)
            src = prefix_ref.at[:, :, lanes((2 * to + other_y) * HD, HD)]
            dst = kv.at[y, 0, :, pl.ds(pl.multiple_of(SPAN_ROWS + g * 16, 16), 16), :]
            if dy == 0 and k == 0:
                copy = pltpu.make_async_copy(src, dst, own_sem.at[0])
            else:
                n = dy * GROUPS + k
                copy = remote(src, dst, pre_send.at[n], pre_recv.at[n], (other_c, to))
                pre_copies.append(copy)
            copy.start()
            if dy == 0 and k == 0:
                pre_own = copy
    query_copy = remote(
        q_ref.at[:, lanes((1 - y) * HALF, HALF)], qs.at[0], pair_send.at[1], pair_recv.at[1], along_y
    )

    def at(z_, x_):
        return z_ * 4 + x_

    def device(p):
        return (2 * p + y, g)

    along_z = (device(at(rem(z + 1, 4), x)), device(at(rem(z + 3, 4), x)))
    along_x = (device(at(z, rem(x + 1, 4))), device(at(z, rem(x + 3, 4))))
    minor = (along_x, along_z)
    major = (along_z, along_x)
    given = {}
    halves = range(2)
    heads = range(2)

    def slot(big, small):
        return big * 4 + small

    def block(e, s, piece):
        return kv.at[e, s] if piece is None else kv.at[e, s, piece : piece + 1]

    def give(e, src, dst, to, piece=None):
        n = len(given)
        given[e, dst, piece] = (n, src)
        remote(block(e, src, piece), block(e, dst, piece), send.at[n], recv.at[n], to).start()

    def take(e, dst, piece=None):
        n, _ = given[e, dst, piece]
        here = block(e, dst, piece)
        remote(here, here, send.at[n], recv.at[n], along_y).wait_recv()

    def both(e, axis, src, dst_next, dst_previous):
        give(e, src, dst_next, axis[e][0])
        give(e, src, dst_previous, axis[e][1])

    def big_step(e, small):
        both(e, major, slot(0, small), slot(3, small), slot(1, small))

    def columns(which):
        return pl.ds(pl.multiple_of(which * width, width), width)

    def rows_of(which, count):
        return pl.ds(pl.multiple_of(which * count, count), count)

    kv_copies = {}

    def exchange(n, pair):
        for k in range(1, GROUPS):
            to = rem(g + k, GROUPS)
            src, dst = pair(to)
            copy = remote(src, dst, kv_send.at[n, k - 1], kv_recv.at[n, k - 1], (c, to))
            copy.start()
            kv_copies[n, k] = copy
        src, dst = pair(g)
        copy = pltpu.make_async_copy(src, dst, own_sem.at[n])
        copy.start()
        kv_copies[n, 0] = copy

    def received(n):
        kv_copies[n, 0].wait()
        for k in range(1, GROUPS):
            kv_copies[n, k].wait_recv()

    exchange(2, lambda to: (private_ref.at[:, :, columns(to)], priv.at[g]))
    query_copy.start()
    exchange(1, lambda to: (span_ref.at[:, rows_of(to, 32), :], relaid_out.at[:, :, columns(g)]))

    span_copy.wait_recv()
    pre_own.wait()
    for copy in pre_copies:
        copy.wait_recv()
    for e in halves:
        both(e, minor, 0, slot(0, 3), slot(0, 1))
    for e in halves:
        big_step(e, 0)

    row = lax.broadcasted_iota(jnp.int32, (SPAN_ROWS, 2 * SPAN_ROWS), 0)
    col = lax.broadcasted_iota(jnp.int32, (SPAN_ROWS, 2 * SPAN_ROWS), 1)
    ones = jnp.ones((SPAN_ROWS, HD), BF16)
    per_tile = TILE // SPAN_ROWS

    def query(t):
        who, first_head = t // (TILES // 2), rem(t, TILES // 2) * per_tile
        return jnp.concatenate(
            [qs[who, :, lanes((first_head + n) * HD, HD)] for n in range(per_tile)], axis=0
        )

    def first(t, carry):
        mine_here = t // (TILES // 2)
        at_y = y * mine_here + (1 - y) * (1 - mine_here)
        allowed = jnp.concatenate([col - SPAN_ROWS * at_y <= row] * per_tile, axis=0)
        keys = jnp.concatenate([kv[0, 0, 0, :SPAN_ROWS, :], kv[1, 0, 0, :SPAN_ROWS, :]], axis=0)
        values = jnp.concatenate(
            [
                jnp.concatenate([kv[0, 0, 1, :SPAN_ROWS, :], ones], axis=1),
                jnp.concatenate([kv[1, 0, 1, :SPAN_ROWS, :], ones], axis=1),
            ],
            axis=0,
        )
        s = jnp.where(allowed, dot_t(query(t), keys) * SCALE, MASKED)
        highest = jnp.broadcast_to(jnp.max(s, axis=1, keepdims=True), (TILE, HD))
        weights = jnp.exp2(s - jnp.concatenate([highest, highest], axis=1)).astype(BF16)
        acc[t] = dot(weights, values)
        top[t] = highest
        return carry

    q_copy.wait()
    lax.fori_loop(TILES // 2, TILES, first, 0)

    for small in (3, 1):
        for e in halves:
            take(e, slot(0, small))
            if small == 3:
                give(e, slot(0, 3), slot(0, 2), minor[e][0], 0)
            else:
                give(e, slot(0, 1), slot(0, 2), minor[e][1], 1)
            big_step(e, small)

    for e in halves:
        take(e, slot(0, 2), 0)
        take(e, slot(0, 2), 1)
        big_step(e, 2)

    qf[...] = jnp.zeros_like(qf)
    dq_copy.wait()
    for j in range(2 * PER):
        start = (j // PER) * SAMPLES * PAD + j % PER
        for level in range(STACK):
            qf[pl.ds(start + level * PAD, PLANE, stride=STACK * PAD), :] = dq_buf[
                level * PLANE : (level + 1) * PLANE, j * HD : (j + 1) * HD
            ].astype(F32)

    def set_suffix(b, carry):
        suf[pl.ds(pl.multiple_of(b * 8, 8), 8), :] = jnp.full((8, HD), suffix_ref[b], jnp.int32)
        return carry

    lax.fori_loop(0, SAMPLES, set_suffix, 0)
    rows = SAMPLES * PAD
    place = lax.broadcasted_iota(jnp.int32, (rows, 2 * HD), 0) >> 4
    key_sample = lax.broadcasted_iota(jnp.int32, (rows, 2 * HD), 1) >> 3
    bias[...] = jnp.where(((place & 3) << 3) + (place >> 2) == key_sample, 0.0, MASKED)

    pre_row = lax.broadcasted_iota(jnp.int32, (PRE_ROWS, HD), 0)

    def put(to_keys, to_values, b, here, ok, key, value, sub):
        count = key.shape[0]
        keep = jnp.where(ok, 1.0, 0.0).astype(BF16)
        drop = jnp.where(ok, 0.0, 1.0).astype(BF16)
        to_keys[b, here : here + count, :] = key * keep + sub * drop
        to_values[b, here : here + count, :HD] = value * keep
        to_values[b, here : here + count, HD:] = keep

    def score(t, b, half):
        q = query(t)
        most = None
        for a in range(0, CHUNK, 2 * HD):
            s = dot_t(q, kp[b, a : a + 2 * HD, :])
            scores[half, :, a : a + 2 * HD] = s
            here = jnp.maximum(s[:, :HD], s[:, HD:])
            most = here if most is None else jnp.maximum(most, here)
        tops[half] = most

    def weigh(t, b, half):
        before = top[t]
        highest = jnp.maximum(
            before, jnp.broadcast_to(jnp.max(tops[half], axis=1, keepdims=True) * SCALE, (TILE, HD))
        )
        rescale = jnp.exp2(before - highest)
        top[t] = highest
        weights = jnp.concatenate(
            [
                jnp.exp2(scores[half, :, a : a + HD] * SCALE - highest).astype(BF16)
                for a in range(0, CHUNK, HD)
            ],
            axis=1,
        )
        acc[t] = acc[t] * jnp.concatenate([rescale, rescale], axis=1) + dot(weights, vp[b, :CHUNK, :])

    def prepare(b, big):
        sub = kv[0, 0, 0, 0:1, :]
        for n in range(4):
            for e in halves:
                dz, dx = (big, n) if e == 0 else (n, big)
                from_pair = at(rem(z + dz, 4), rem(x + dx, 4))
                s = slot(big, n)
                span_ok = jnp.full((SPAN_ROWS, HD), from_pair, jnp.int32) < pair
                pre_ok = (2 * from_pair + e) * PRE_ROWS + pre_row < limit
                here = (2 * n + e) * ROWS
                put(kp, vp, b, here, span_ok, kv[e, s, 0, :SPAN_ROWS, :], kv[e, s, 1, :SPAN_ROWS, :], sub)
                put(kp, vp, b, here + SPAN_ROWS, pre_ok, kv[e, s, 0, SPAN_ROWS:, :], kv[e, s, 1, SPAN_ROWS:, :], sub)

    def run(steps, tile_of, chunk_of):
        def scored(i, half):
            score(tile_of(i), chunk_of(i), half)

        def weighed(i, half):
            weigh(tile_of(i), chunk_of(i), half)

        def two(i, carry):
            scored(2 * i + 1, 1)
            weighed(2 * i, 0)
            scored(2 * i + 2, 0)
            weighed(2 * i + 1, 1)
            return carry

        scored(0, 0)
        lax.fori_loop(0, (steps - 1) // 2, two, 0)
        if steps % 2 == 0:
            scored(steps - 1, 1)
            weighed(steps - 2, 0)
            weighed(steps - 1, 1)
        else:
            weighed(steps - 1, 0)

    def pass_on(*smalls):
        for small in smalls:
            for e in halves:
                if small in (0, 1):
                    take(e, slot(3, small))
                    give(e, slot(3, small), slot(2, small), major[e][0])
                else:
                    take(e, slot(1, small))
                    give(e, slot(1, small), slot(2, small), major[e][1])

    half_tiles = TILES // 2

    def mates(i):
        return rem(i, half_tiles)

    def own(i):
        return half_tiles + rem(i, half_tiles)

    def which(i):
        return i // half_tiles

    prepare(0, 0)
    run(half_tiles, own, lambda i: 0)

    pass_on(0, 3)
    pass_on(1, 2)
    for e in halves:
        take(e, slot(3, 3))
        take(e, slot(3, 2))
    prepare(1, 3)
    run(half_tiles, own, lambda i: 1)

    def message(sums, lse):
        high = [v.astype(BF16).astype(F32) for v in lse]
        middle = [(v - w).astype(BF16).astype(F32) for v, w in zip(lse, high)]
        low = [v - w - u for v, w, u in zip(lse, high, middle)]
        lane = lax.broadcasted_iota(jnp.int32, sums[0].shape, sums[0].ndim - 1)
        stats = jnp.zeros(sums[0].shape, F32)
        for h in heads:
            for n, piece in enumerate((high[h], middle[h], low[h])):
                stats = jnp.where(lane == 3 * h + n, piece, stats)
        return [sums[0].astype(BF16), sums[1].astype(BF16), stats.astype(BF16)]

    def merge(stat, sums, h):
        lse = stat[..., 3 * h : 3 * h + 1] + stat[..., 3 * h + 1 : 3 * h + 2] + stat[..., 3 * h + 2 : 3 * h + 3]
        most = jnp.max(lse, axis=0, keepdims=True)
        weight = jnp.exp2(lse - most)
        total = jnp.sum(weight, axis=0)
        return jnp.sum(weight * sums.astype(F32), axis=0) / total

    received(2)
    row_in = lax.broadcasted_iota(jnp.int32, (8 * SAMPLES, HD), 0) & 7
    partial, partial_lse = [], []
    for h in heads:
        cols = slice(h * HD, (h + 1) * HD)
        sub = span_ref[0, 0:1, cols]
        held = jnp.full((SPAN_ROWS, HD), y, jnp.int32) == h
        for e in halves:
            pre_ok = (2 * pair + e) * PRE_ROWS + pre_row < jnp.where(y == h, limit, 0)
            put(dk, dv, h, e * ROWS, held, kv[e, 0, 0, :SPAN_ROWS, :], kv[e, 0, 1, :SPAN_ROWS, :], sub)
            put(dk, dv, h, e * ROWS + SPAN_ROWS, pre_ok, kv[e, 0, 0, SPAN_ROWS:, :], kv[e, 0, 1, SPAN_ROWS:, :], sub)
        for s in range(GROUPS):
            ok = (c * GROUPS + s) * 8 + row_in < suf[...]
            put(dk, dv, h, 2 * ROWS + s * 8 * SAMPLES, ok, priv[s, 0, :, cols], priv[s, 1, :, cols], sub)
        q = qf[h * rows : (h + 1) * rows, :].astype(BF16)
        most = None
        for start, count in [(a, HD) for a in range(0, 2 * ROWS, HD)] + [(2 * ROWS + s * 256, 256) for s in range(GROUPS)]:
            s = dot_t(q, dk[h, start : start + count, :]) * SCALE
            if count == 256:
                s = s + bias[...]
            scores[h, :, start : start + count] = s
            here = jnp.maximum(s[:, :HD], s[:, HD:]) if count == 256 else s
            most = here if most is None else jnp.maximum(most, here)
        most = jnp.broadcast_to(jnp.max(most, axis=1, keepdims=True), (rows, HD))
        weights = jnp.concatenate(
            [jnp.exp2(scores[h, :, a : a + HD] - most).astype(BF16) for a in range(0, TOTAL, HD)], axis=1
        )
        both_sums = dot(weights, dv[h, :TOTAL, :])
        sum_here = jnp.maximum(both_sums[:, HD:], LEAST)
        partial.append(both_sums[:, :HD] / sum_here)
        partial_lse.append(most + jnp.log2(sum_here))
    for n, piece in enumerate(message(partial, partial_lse)):
        msg[:, n, :, :] = piece.reshape(SAMPLES, PAD, HD)

    def place_of(ctx):
        return rem(ctx, PLANE) * STACK + ctx // PLANE

    def in_copy(k):
        to = rem(c + k, CTX)
        return remote(msg.at[place_of(to)], inbox.at[k], ex_send.at[0], ex_recv.at[0], (to, g))

    def mix_copy(k):
        to = rem(c + k, CTX)
        return remote(mix_own, mix_all.at[place_of(c)], ex_send.at[1], ex_recv.at[1], (to, g))

    def every(act):
        def one(k, carry):
            act(k)
            return carry

        lax.fori_loop(1, CTX, one, 0)

    every(lambda k: in_copy(k).start())
    inbox[0] = msg[place_of(c)]

    query_copy.wait_recv()
    lax.fori_loop(0, half_tiles, first, 0)
    run(TILES, mates, which)

    others = inbox.at[1:]
    remote(others, others, ex_send.at[0], ex_recv.at[0], along_y).wait()
    stat = inbox[:, 2, :, :].astype(F32)
    for h in heads:
        mix_own[h] = merge(stat, inbox[:, h, :, :], h).astype(BF16)
    every(lambda k: mix_copy(k).start())
    mix_all[place_of(c)] = mix_own[...]

    for e in halves:
        for small in range(4):
            if small < 2:
                take(e, slot(1, small))
            take(e, slot(2, small))
    prepare(0, 1)
    prepare(1, 2)
    run(TILES, mates, which)

    for j in range(PER):
        t, r = j * SPAN_ROWS // TILE, j * SPAN_ROWS % TILE
        here = slice(r, r + SPAN_ROWS)
        back[:, j * HD : (j + 1) * HD] = (acc[t, here, :HD] / acc[t, here, HD:]).astype(BF16)
    back_copy = remote(back, back_in, pair_send.at[2], pair_recv.at[2], along_y)
    back_copy.start()

    others = mix_all.at[1:]
    remote(others, others, ex_send.at[1], ex_recv.at[1], along_y).wait()
    mix_f[...] = mix_all[...].astype(F32).reshape(SAMPLES * 2 * PAD, HD)
    w_copy.wait()
    product = jnp.zeros((SAMPLES, w_buf.shape[1]), F32)
    for j in range(2 * PER):
        start = (j // PER) * PAD + j % PER
        a = jnp.concatenate(
            [
                mix_f[pl.ds(start + n * 2 * PAD, PLANE, stride=STACK * 2 * PAD), :]
                for n in range(STACK)
            ],
            axis=0,
        ).astype(BF16)
        product = product + dot(a, w_buf[j * HD : (j + 1) * HD, :])
    part[...] = product
    part_copies = []
    for k in range(1, GROUPS):
        to = rem(g + k, GROUPS)
        copy = remote(part, parts.at[g], part_send.at[k - 1], part_recv.at[k - 1], (c, to))
        copy.start()
        part_copies.append(copy)
    parts[g] = product

    run(TILES, own, which)

    for j in range(PER):
        t, r = half_tiles + j * SPAN_ROWS // TILE, j * SPAN_ROWS % TILE
        here = slice(r, r + SPAN_ROWS)
        out_ref[:, lanes(y * HALF + j * HD, HD)] = acc[t, here, :HD] / acc[t, here, HD:]
    back_copy.wait()
    out_ref[:, lanes((1 - y) * HALF, HALF)] = back_in[...].astype(F32)

    for copy in part_copies:
        copy.wait()
    decode_out[...] = (parts[0] + parts[1]) + (parts[2] + parts[3])
    received(1)
    for (n, k), copy in kv_copies.items():
        if k:
            copy.wait_send()
    span_copy.wait_send()
    query_copy.wait_send()
    for copy in pre_copies:
        copy.wait_send()
    for (e, _, piece), (n, src) in given.items():
        there = block(e, src, piece)
        remote(there, there, send.at[n], recv.at[n], along_y).wait_send()


def shards(
    span_queries,
    span_keyvals,
    prefix_keyvals,
    offset,
    decode_queries,
    private_keyvals,
    suffix_lengths,
    out_weight,
):
    vmem = pl.BlockSpec(memory_space=pltpu.VMEM)
    smem = pl.BlockSpec(memory_space=pltpu.SMEM)
    hbm = pl.BlockSpec(memory_space=pl.ANY)
    dma = pltpu.SemaphoreType.DMA
    group = 2 * PER * HD
    wide = out_weight.shape[1]
    private = private_keyvals.reshape(2, SAMPLES * 8, KVH * HD)
    return pl.pallas_call(
        kernel,
        out_shape=(
            jax.ShapeDtypeStruct((SPAN_ROWS, group), F32),
            jax.ShapeDtypeStruct((2, SPAN_ROWS // GROUPS, KVH * HD), BF16),
            jax.ShapeDtypeStruct((SAMPLES, wide), F32),
        ),
        in_specs=[smem, smem, hbm, vmem, vmem, hbm, hbm, hbm],
        out_specs=(vmem, vmem, vmem),
        scratch_shapes=[
            pltpu.VMEM((2, CTX // 2, 2, ROWS, HD), BF16),
            pltpu.VMEM((2, CHUNK, HD), BF16),
            pltpu.VMEM((2, CHUNK, 2 * HD), BF16),
            pltpu.VMEM((2, TOTAL, HD), BF16),
            pltpu.VMEM((2, TOTAL, 2 * HD), BF16),
            pltpu.VMEM((TILES, TILE, 2 * HD), F32),
            pltpu.VMEM((TILES, TILE, HD), F32),
            pltpu.VMEM((2, TILE, CHUNK), F32),
            pltpu.VMEM((2, TILE, HD), F32),
            pltpu.VMEM((2, SPAN_ROWS, group // 2), BF16),
            pltpu.VMEM((SPAN_ROWS, group // 2), BF16),
            pltpu.VMEM((SPAN_ROWS, group // 2), BF16),
            pltpu.VMEM((group, wide), BF16),
            pltpu.VMEM((SAMPLES, group), BF16),
            pltpu.VMEM((2 * SAMPLES * PAD, HD), F32),
            pltpu.VMEM((GROUPS, 2, SAMPLES * 8, 2 * HD), BF16),
            pltpu.VMEM((SAMPLES * 8, HD), jnp.int32),
            pltpu.VMEM((SAMPLES * PAD, 2 * HD), F32),
            pltpu.VMEM((SAMPLES, 3, PAD, HD), BF16),
            pltpu.VMEM((CTX, 3, PAD, HD), BF16),
            pltpu.VMEM((2, PAD, HD), BF16),
            pltpu.VMEM((SAMPLES, 2, PAD, HD), BF16),
            pltpu.VMEM((SAMPLES * 2 * PAD, HD), F32),
            pltpu.VMEM((SAMPLES, wide), F32),
            pltpu.VMEM((GROUPS, SAMPLES, wide), F32),
            dma((40,)), dma((40,)), dma((3,)),
            dma((3, GROUPS - 1)), dma((3, GROUPS - 1)), dma((3,)),
            dma((2 * GROUPS,)), dma((2 * GROUPS,)), dma((3,)), dma((3,)),
            dma((2,)), dma((2,)), dma((GROUPS - 1,)), dma((GROUPS - 1,)),
        ],
        compiler_params=pltpu.CompilerParams(
            collective_id=0, has_side_effects=True, vmem_limit_bytes=60 * 1024 * 1024
        ),
        name="attention",
    )(offset, suffix_lengths, span_queries, span_keyvals, prefix_keyvals, private, decode_queries, out_weight)


def solution(mesh):
    return jax.shard_map(
        shards,
        mesh=mesh,
        in_specs=(
            P("ctx", "kvh"),
            P(None, "ctx", "kvh"),
            P(None, ("ctx", "kvh"), None),
            P(),
            P(),
            P(None, None, ("ctx", "kvh"), None),
            P(),
            P("kvh", "ctx"),
        ),
        out_specs=(P("ctx", "kvh"), P(None, ("ctx", "kvh"), None), P(None, "ctx")),
        check_vma=False,
    )
```

time: 76.5 us -> 71.5 us (0.935); the launches traced: 76.4 us -> 70.1 us
  Pallas kernels: 71 us -> 64.8 us
    pallas_call x1, Pallas kernels: 71 us -> 64.8 us  [shards(): pl.pallas_call(kernel, out_shape=(jax.ShapeDtypeStruct((SPAN_ROWS, group)...]
where the time goes in v3:
time: 71.5 us; the launch traced here: 70.1 us
  Pallas kernels  64.8 us (91%)
  local copies, waits for them, and re-layouts  4.02 us (6%)
  between operations  1.3 us (2%)
    pallas_call x1, Pallas kernels, shards(): pl.pallas_call(kernel, out_shape=(jax.ShapeDtypeStruct((SPAN_ROWS, group)...  64.8 us
    unnamed x7, local copies, waits for them, and re-layouts  4.02 us

profile of v3, /device:TPU:0, one launch (start us, length us, event | category | flops | bytes accessed | tf_op | source)
XLA Modules:
  0.0 70.1 jit_solution(10584861931252473000)
XLA Ops:
  1.3 64.8 %attention.1 = (f32[128,3072]{1,0:T(8,128)}, bf16[2,32,1024]{2,1,0:T(8,128)(2,1)}, f32[32,384]{1,0:T(8,128)}) custom-call(s32[1]{0:T(128)S(6)} %copy.14.limit_ref, s32[32]{0:T(128)} %suffix_ref.1, bf16[128,3072]{1,0:T(8,128)(2,1)} %q_ref.1, bf16[2,128,256]{2,1,0:T(8,128)(2,1)} %span_ref.1, bf16[2,16,1024]{2,1,0:T(8,128)(2,1)} %prefix_ref.1, ...), custom_call_target="tpu_custom_call" | custom-call | tf_op jit(solution)/shard_map/attention/pallas_call | solution.py:532
  66.1 0.0 copy-start
  66.1 0.0 copy-start.1
  66.1 2.7 %copy.15 = f32[128,3072]{1,0:T(8,128)} copy(f32[128,3072]{1,0:T(8,128)} %get-tuple-element.6) | data formatting | bytes 3145728
  68.8 0.0 copy-done
  68.8 0.7 copy.16
  69.5 0.0 copy-done.1
  69.5 0.6 copy.17
Async XLA Ops:
  66.1 2.8 %copy-start = (bf16[2,32,1024]{2,1,0:T(8,128)(2,1)S(1)}, bf16[2,32,1024]{2,1,0:T(8,128)(2,1)}, u32[]{:S(2)}) copy-start(bf16[2,32,1024]{2,1,0:T(8,128)(2,1)} %get-tuple-element.7) | copy-start | bytes 393220
  66.1 3.4 %copy-start.1 = (f32[32,384]{1,0:T(8,128)S(1)}, f32[32,384]{1,0:T(8,128)}, u32[]{:S(2)}) copy-start(f32[32,384]{1,0:T(8,128)} %get-tuple-element.8) | copy-start | bytes 147460

commit v4 on v3

--- a/solution.py
+++ b/solution.py
@@ -21,7 +21,7 @@
 SCALE = HD ** (-0.5) * LOG2E
 MASKED = -1e30
 LEAST = 2.0**-100
-TILE = 512
+TILE = 768
 TILES = 2 * PER * SPAN_ROWS // TILE
 CHUNK = 8 * ROWS
 HALF = PER * HD
@@ -55,7 +55,7 @@
 def kernel(
     limit_ref, suffix_ref, q_ref, span_ref, prefix_ref, private_ref, dq_ref, w_ref,
     out_ref, relaid_out, decode_out,
-    kv, kp, vp, dk, dv, acc, top, scores, tops, qs, back, back_in,
+    kv, kp, vp, dk, dv, acc, top, scores, tops, qs, back,
     w_buf, dq_buf, qf, priv, suf, bias, msg, inbox, mix_own, mix_all, mix_f, part, parts,
     send, recv, local, kv_send, kv_recv, own_sem, pre_send, pre_recv, pair_send, pair_recv,
     ex_send, ex_recv, part_send, part_recv,
@@ -93,11 +93,6 @@
     pl.semaphore_wait(barrier, 2 * (GROUPS - 1) + CTX - 1)
 
     along_y = (mate, g)
-    span_copy = remote(
-        span_ref.at[:, :, lanes((1 - y) * HD, HD)], kv.at[y, 0, :, :SPAN_ROWS, :],
-        pair_send.at[0], pair_recv.at[0], along_y,
-    )
-    span_copy.start()
     pre_copies = []
     for dy, other_y, other_c in ((1, 1 - y, mate), (0, y, c)):
         for k in range(GROUPS):
@@ -113,6 +108,11 @@
             copy.start()
             if dy == 0 and k == 0:
                 pre_own = copy
+    span_copy = remote(
+        span_ref.at[:, :, lanes((1 - y) * HD, HD)], kv.at[y, 0, :, :SPAN_ROWS, :],
+        pair_send.at[0], pair_recv.at[0], along_y,
+    )
+    span_copy.start()
     query_copy = remote(
         q_ref.at[:, lanes((1 - y) * HALF, HALF)], qs.at[0], pair_send.at[1], pair_recv.at[1], along_y
     )
@@ -239,25 +239,6 @@
         take(e, slot(0, 2), 1)
         big_step(e, 2)
 
-    qf[...] = jnp.zeros_like(qf)
-    dq_copy.wait()
-    for j in range(2 * PER):
-        start = (j // PER) * SAMPLES * PAD + j % PER
-        for level in range(STACK):
-            qf[pl.ds(start + level * PAD, PLANE, stride=STACK * PAD), :] = dq_buf[
-                level * PLANE : (level + 1) * PLANE, j * HD : (j + 1) * HD
-            ].astype(F32)
-
-    def set_suffix(b, carry):
-        suf[pl.ds(pl.multiple_of(b * 8, 8), 8), :] = jnp.full((8, HD), suffix_ref[b], jnp.int32)
-        return carry
-
-    lax.fori_loop(0, SAMPLES, set_suffix, 0)
-    rows = SAMPLES * PAD
-    place = lax.broadcasted_iota(jnp.int32, (rows, 2 * HD), 0) >> 4
-    key_sample = lax.broadcasted_iota(jnp.int32, (rows, 2 * HD), 1) >> 3
-    bias[...] = jnp.where(((place & 3) << 3) + (place >> 2) == key_sample, 0.0, MASKED)
-
     pre_row = lax.broadcasted_iota(jnp.int32, (PRE_ROWS, HD), 0)
 
     def put(to_keys, to_values, b, here, ok, key, value, sub):
@@ -355,6 +336,26 @@
     run(half_tiles, own, lambda i: 0)
 
     pass_on(0, 3)
+
+    qf[...] = jnp.zeros_like(qf)
+    dq_copy.wait()
+    for j in range(2 * PER):
+        start = (j // PER) * SAMPLES * PAD + j % PER
+        for level in range(STACK):
+            qf[pl.ds(start + level * PAD, PLANE, stride=STACK * PAD), :] = dq_buf[
+                level * PLANE : (level + 1) * PLANE, j * HD : (j + 1) * HD
+            ].astype(F32)
+
+    def set_suffix(b, carry):
+        suf[pl.ds(pl.multiple_of(b * 8, 8), 8), :] = jnp.full((8, HD), suffix_ref[b], jnp.int32)
+        return carry
+
+    lax.fori_loop(0, SAMPLES, set_suffix, 0)
+    rows = SAMPLES * PAD
+    place = lax.broadcasted_iota(jnp.int32, (rows, 2 * HD), 0) >> 4
+    key_sample = lax.broadcasted_iota(jnp.int32, (rows, 2 * HD), 1) >> 3
+    bias[...] = jnp.where(((place & 3) << 3) + (place >> 2) == key_sample, 0.0, MASKED)
+
     pass_on(1, 2)
     for e in halves:
         take(e, slot(3, 3))
@@ -400,12 +401,12 @@
             s = dot_t(q, dk[h, start : start + count, :]) * SCALE
             if count == 256:
                 s = s + bias[...]
-            scores[h, :, start : start + count] = s
+            scores[h, :rows, start : start + count] = s
             here = jnp.maximum(s[:, :HD], s[:, HD:]) if count == 256 else s
             most = here if most is None else jnp.maximum(most, here)
         most = jnp.broadcast_to(jnp.max(most, axis=1, keepdims=True), (rows, HD))
         weights = jnp.concatenate(
-            [jnp.exp2(scores[h, :, a : a + HD] - most).astype(BF16) for a in range(0, TOTAL, HD)], axis=1
+            [jnp.exp2(scores[h, :rows, a : a + HD] - most).astype(BF16) for a in range(0, TOTAL, HD)], axis=1
         )
         both_sums = dot(weights, dv[h, :TOTAL, :])
         sum_here = jnp.maximum(both_sums[:, HD:], LEAST)
@@ -460,7 +461,7 @@
         t, r = j * SPAN_ROWS // TILE, j * SPAN_ROWS % TILE
         here = slice(r, r + SPAN_ROWS)
         back[:, j * HD : (j + 1) * HD] = (acc[t, here, :HD] / acc[t, here, HD:]).astype(BF16)
-    back_copy = remote(back, back_in, pair_send.at[2], pair_recv.at[2], along_y)
+    back_copy = remote(back, out_ref.at[:, lanes(y * HALF, HALF)], pair_send.at[2], pair_recv.at[2], along_y)
     back_copy.start()
 
     others = mix_all.at[1:]
@@ -492,9 +493,8 @@
     for j in range(PER):
         t, r = half_tiles + j * SPAN_ROWS // TILE, j * SPAN_ROWS % TILE
         here = slice(r, r + SPAN_ROWS)
-        out_ref[:, lanes(y * HALF + j * HD, HD)] = acc[t, here, :HD] / acc[t, here, HD:]
+        out_ref[:, lanes(y * HALF + j * HD, HD)] = (acc[t, here, :HD] / acc[t, here, HD:]).astype(BF16)
     back_copy.wait()
-    out_ref[:, lanes((1 - y) * HALF, HALF)] = back_in[...].astype(F32)
 
     for copy in part_copies:
         copy.wait()
@@ -529,10 +529,10 @@
     group = 2 * PER * HD
     wide = out_weight.shape[1]
     private = private_keyvals.reshape(2, SAMPLES * 8, KVH * HD)
-    return pl.pallas_call(
+    span_attention, relaid_span, decode_output = pl.pallas_call(
         kernel,
         out_shape=(
-            jax.ShapeDtypeStruct((SPAN_ROWS, group), F32),
+            jax.ShapeDtypeStruct((SPAN_ROWS, group), BF16),
             jax.ShapeDtypeStruct((2, SPAN_ROWS // GROUPS, KVH * HD), BF16),
             jax.ShapeDtypeStruct((SAMPLES, wide), F32),
         ),
@@ -549,7 +549,6 @@
             pltpu.VMEM((2, TILE, CHUNK), F32),
             pltpu.VMEM((2, TILE, HD), F32),
             pltpu.VMEM((2, SPAN_ROWS, group // 2), BF16),
-            pltpu.VMEM((SPAN_ROWS, group // 2), BF16),
             pltpu.VMEM((SPAN_ROWS, group // 2), BF16),
             pltpu.VMEM((group, wide), BF16),
             pltpu.VMEM((SAMPLES, group), BF16),
@@ -574,6 +573,7 @@
         ),
         name="attention",
     )(offset, suffix_lengths, span_queries, span_keyvals, prefix_keyvals, private, decode_queries, out_weight)
+    return (span_attention.astype(F32), relaid_span, decode_output)
 
 
 def solution(mesh):

time: 71.5 us -> 67.7 us (0.947)
  the two profiles are of different devices: /device:TPU:0 before, /device:TPU:1 now
where the time goes in v4:
time: 67.7 us; the launch traced here: 67.5 us
  Pallas kernels  62.5 us (92%)
  other arithmetic  2.46 us (4%)
  between operations  1.3 us (2%)
  local copies, waits for them, and re-layouts  1.28 us (2%)
    pallas_call x1, Pallas kernels, shards(): pl.pallas_call(kernel, out_shape=(jax.ShapeDtypeStruct((SPAN_ROWS, group)...  62.5 us
    convert_element_type x1, other arithmetic, shards(): return (span_attention.astype(F32), relaid_span, decode_output)  2.46 us

profile of v4, /device:TPU:1, one launch (start us, length us, event | category | flops | bytes accessed | tf_op | source)
XLA Modules:
  0.0 67.5 jit_solution(778813009912244159)
XLA Ops:
  1.3 62.5 %attention.1 = (bf16[128,3072]{1,0:T(8,128)(2,1)}, bf16[2,32,1024]{2,1,0:T(8,128)(2,1)}, f32[32,384]{1,0:T(8,128)}) custom-call(s32[1]{0:T(128)S(6)} %copy.13.limit_ref, s32[32]{0:T(128)} %suffix_ref.1, bf16[128,3072]{1,0:T(8,128)(2,1)} %q_ref.1, bf16[2,128,256]{2,1,0:T(8,128)(2,1)} %span_ref.1, bf16[2,16,1024]{2,1,0:T(8,128)(2,1)} %prefix_ref.1, ...), custom_call_target="tpu_custom_call" | custom-call | tf_op jit(solution)/shard_map/attention/pallas_call | solution.py:532
  63.7 0.0 copy-start
  63.7 0.0 copy-start.1
  63.8 2.5 %convert_element_type.3 = f32[128,3072]{1,0:T(8,128)} convert(bf16[128,3072]{1,0:T(8,128)(2,1)} %get-tuple-element.6) | non-fusion elementwise | flops 393216 | bytes 2359296 | tf_op jit(solution)/shard_map/convert_element_type | solution.py:576
  66.2 0.0 copy-done
  66.2 0.7 copy.14
  66.9 0.0 copy-done.1
  66.9 0.6 copy.15
Async XLA Ops:
  63.7 2.5 %copy-start = (bf16[2,32,1024]{2,1,0:T(8,128)(2,1)S(1)}, bf16[2,32,1024]{2,1,0:T(8,128)(2,1)}, u32[]{:S(2)}) copy-start(bf16[2,32,1024]{2,1,0:T(8,128)(2,1)} %get-tuple-element.13) | copy-start | bytes 393220
  63.7 3.1 %copy-start.1 = (f32[32,384]{1,0:T(8,128)S(1)}, f32[32,384]{1,0:T(8,128)}, u32[]{:S(2)}) copy-start(f32[32,384]{1,0:T(8,128)} %get-tuple-element.14) | copy-start | bytes 147460
